TPU v7x, 512 devices: a whole 4x4x16 slice. The times are simulated.
512 devices in a mesh: grp: 4 (over z_lo), gx: 16 (over y, x), gy: 8 (over z_hi, core).
Axes of the slice: x: 4, y: 4, z: 16 (z_hi: 4, z_lo: 4; z = z_hi * 4 + z_lo), core: 2. Of those that a mesh axis runs over, the one named last changes fastest.
Arguments:
- fields: float32 [4, 6, 2, 256, 1024], P('grp', None, None, 'gx', 'gy'), may hold values from -6 to 6
- stored: bfloat16 [4, 2, 6, 2, 256, 1024], P('grp', None, None, None, 'gx', 'gy'), may hold values from -6 to 6
- material: int32 [2, 256, 1024], P(None, 'gx', 'gy'), may hold values from 0 to 3
- design: float32 [256, 1024], P('gx', 'gy'), may hold values from 0 to 2
- mat_eps: float32 [4], replicated, may hold values from 1 to 4
- mat_chi: float32 [4], replicated, may hold values from 0.05 to 0.4
- source_wave: float32 [2, 4], replicated, may hold values from -4 to 4
- source_cells: int32 [2048], replicated, may hold values from 0 to 524287
- monitor_cells: int32 [2048], replicated, may hold values from 0 to 524287
- owners: int32 [2048], replicated, may hold values from 0 to 2047, each once
Outputs:
- fields_next: float32 [4, 6, 2, 256, 1024], P('grp', None, None, 'gx', 'gy')
- stored_next: bfloat16 [4, 2, 6, 2, 256, 1024], P('grp', None, None, None, 'gx', 'gy')
- design_grad: float32 [2048, 128], P(('grp', 'gx', 'gy'))
Inputs may be any that keep to these rules, and one draw needn't show every extreme that they name: owners names every row of design_grad exactly once.
All inputs are finite; a program needn't handle non-finite values.
Results may differ from a plain program's by a relative error of at most 0.00105.
Values may be sent and summed in bfloat16 or wider, within the bound.
A program may use at most 64 MiB of HBM per device.

v0:
```python
import jax
import jax.numpy as jnp
from jax import lax
from jax.sharding import PartitionSpec as P

STEPS = 4


time_step = 0.5


def shifted_2(block, axis, distance):
    devices = range(lax.axis_size(axis))
    route = [(i - distance, i) for i in devices if i - distance in devices]
    return lax.ppermute(block, axis, route)


def lookup(material, entries):
    looked_up = jnp.zeros(material.shape, jnp.float32)
    for k in range(entries.shape[0]):
        looked_up = looked_up + jnp.where(material == k, entries[k], 0.0)
    return looked_up


def shifted(values, axis, border, upward):
    length = values.shape[axis]
    if upward:
        interior = lax.slice_in_dim(values, 1, length, axis=axis)
        return jnp.concatenate([interior, border], axis=axis) - values
    interior = lax.slice_in_dim(values, 0, length - 1, axis=axis)
    return values - jnp.concatenate([border, interior], axis=axis)


def curl_of(values, rim_x, rim_y, upward):
    flat_border = jnp.zeros_like(values[0][:1])

    def along_z(c):
        return shifted(values[c], 0, flat_border, upward)

    def along_x(c, border):
        return shifted(values[c], 1, border[:, None, :], upward)

    def along_y(c, border):
        return shifted(values[c], 2, border[:, :, None], upward)

    x_part = along_y(2, rim_y[1]) - along_z(1)
    y_part = along_z(0) - along_x(2, rim_x[1])
    z_part = along_x(1, rim_x[0]) - along_y(0, rim_y[0])
    return jnp.stack([x_part, y_part, z_part])


def boundary_rims(values, layer, offset):
    edge_x = values[1:3, :, layer, :]
    edge_y = values[0::2, :, :, layer]
    return (shifted_2(edge_x, "gx", offset), shifted_2(edge_y, "gy", offset))


def hand_over(snapshots):
    return shifted_2(snapshots, "grp", 2)


def local_slots(cell_ids, z_cells, x_cells, y_cells, total_x, total_y):
    plane_cells = total_x * total_y
    depth_index = cell_ids // plane_cells
    within = cell_ids % plane_cells
    local_x = within // total_y - lax.axis_index("gx") * x_cells
    local_y = within % total_y - lax.axis_index("gy") * y_cells
    inside = (local_x >= 0) & (local_x < x_cells) & (local_y >= 0) & (local_y < y_cells)
    return jnp.where(
        inside, (depth_index * x_cells + local_x) * y_cells + local_y, z_cells * x_cells * y_cells
    )


def local(
    fields,
    stored,
    material,
    design,
    mat_eps,
    mat_chi,
    source_wave,
    source_cells,
    monitor_cells,
    owners,
):
    z_cells, x_cells, y_cells = (fields.shape[2], fields.shape[3], fields.shape[4])
    total_x = x_cells * lax.axis_size("gx")
    total_y = y_cells * lax.axis_size("gy")
    cell_count = z_cells * x_cells * y_cells
    lane_index = lax.axis_index("grp")
    forward = lane_index < 2
    active = jnp.where(forward, 0.0, 1.0)
    source = lane_index % 2
    permittivity = lookup(material, mat_eps) + design[None]
    kerr_chi = lookup(material, mat_chi)
    source_slots = local_slots(source_cells, z_cells, x_cells, y_cells, total_x, total_y)
    monitor_slots = local_slots(monitor_cells, z_cells, x_cells, y_cells, total_x, total_y)
    monitor_read = jnp.minimum(monitor_slots, cell_count - 1)
    magnetic_sign = jnp.where(forward, -time_step, 1.0)
    electric = fields[0, :3]
    magnetic = fields[0, 3:]
    own_half = stored[0]
    halves = STEPS // 2
    gradient = jnp.zeros((x_cells, y_cells), jnp.float32)
    kept_records = []
    outgoing = []
    arrived = hand_over(own_half)
    incoming = [arrived[k] for k in range(halves)]
    for i in range(STEPS):
        if i < halves:
            snapshot = own_half[halves - 1 - i]
        else:
            snapshot = incoming[STEPS - 1 - i]
        wave_value = source_wave[source, i] * (1.0 - active)
        advance_magnetic = magnetic
        past_field = snapshot[:3].astype(jnp.float32)
        curled = snapshot[3:].astype(jnp.float32)
        reference_field = jnp.where(forward, electric, past_field)
        factor = time_step / (
            permittivity + kerr_chi * jnp.sum(reference_field * reference_field, axis=0)
        )
        weighted = jnp.where(forward, electric, factor * electric)
        upper_x, upper_y = boundary_rims(weighted, 0, -1)
        advance_magnetic = advance_magnetic + magnetic_sign * curl_of(
            weighted, upper_x, upper_y, True
        )
        lower_x, lower_y = boundary_rims(advance_magnetic, -1, 1)
        rotated = curl_of(advance_magnetic, lower_x, lower_y, False)
        contracted = jnp.sum(curled * electric, axis=0)
        kerr_term = -2.0 / time_step * kerr_chi * factor * factor * contracted * reference_field
        updated = jnp.where(
            forward, electric + factor * rotated, electric + kerr_term - time_step * rotated
        )
        record = jnp.concatenate([electric, rotated]).astype(jnp.bfloat16)
        flat_field = updated.reshape(3, cell_count).at[0, source_slots].add(wave_value, mode="drop")
        monitor_values = past_field.reshape(3, cell_count)[:, monitor_read] * active
        flat_field = flat_field.at[:, monitor_slots].add(monitor_values, mode="drop")
        grad_term = jnp.sum(-(factor * factor / time_step) * contracted, axis=0) * active
        electric, magnetic, record, grad_term = (
            flat_field.reshape(3, z_cells, x_cells, y_cells),
            advance_magnetic,
            record,
            grad_term,
        )
        gradient = gradient + grad_term
        if i < halves:
            kept_records.append(record)
        else:
            outgoing.append(record)
    handed_over = hand_over(jnp.stack(outgoing))
    stored_next = jnp.where(forward, jnp.stack(kept_records), handed_over)[None]
    fields_next = jnp.concatenate([electric, magnetic])[None]
    tile_ids = (
        lax.axis_index("gx") * x_cells + jnp.arange(x_cells, dtype=jnp.int32)
    ) * lax.axis_size("gy") + lax.axis_index("gy")
    targets = owners[tile_ids]
    spread = jnp.zeros((owners.shape[0], y_cells), jnp.float32).at[targets].set(gradient)
    design_grad = lax.psum_scatter(spread, ("grp", "gx", "gy"), scatter_dimension=0, tiled=True)
    return (fields_next, stored_next, design_grad)


def solution(mesh):
    in_specs = (
        P("grp", None, None, "gx", "gy"),
        P("grp", None, None, None, "gx", "gy"),
        P(None, "gx", "gy"),
        P("gx", "gy"),
        P(),
        P(),
        P(),
        P(),
        P(),
        P(),
    )
    out_specs = (
        P("grp", None, None, "gx", "gy"),
        P("grp", None, None, None, "gx", "gy"),
        P(("grp", "gx", "gy"), None),
    )
    return jax.shard_map(local, mesh=mesh, in_specs=in_specs, out_specs=out_specs, check_vma=False)
```

profile of v0, /device:TPU:1, one launch (start us, length us, event | category | flops | bytes accessed | tf_op | source)
XLA Modules:
  0.0 932.6 jit_solution(11276874804864221973)
XLA Ops:
  11.8 5.7 multiply_reduce_fusion.6
  17.7 8.8 collective-permute-start
  42.7 2.5 fusion.26
  46.1 7.2 collective-permute-start.2
  53.3 4.3 collective-permute-start.3
  59.8 11.5 %scatter_fusion = f32[12288]{0:T(1024)S(1)} fusion(f32[12288]{0:T(1024)S(1)} %reshape.470, s32[2048]{0:T(1024)S(1)} %broadcast_select_fusion.4, f32[2048]{0:T(1024)S(1)} %broadcast.234), kind=kCustom, calls=%fused_computation.10 | custom fusion | flops 2048 | bytes 32768
  72.0 89.0 %scatter_custom_fusion = f32[3,4096]{0,1:T(8,128)S(1)} fusion(f32[3,4096]{0,1:T(8,128)S(1)} %copy.815, s32[2048]{0:T(1024)S(1)} %compare_select_fusion.1, f32[]{:T(128)S(6)} %select_n.220, f32[3,4096]{0,1:T(8,128)} %copy.814, s32[2048]{0:T(1024)S(1)} %get-tuple-element.59), kind=kCustom, calls=%fused_computation.26 | custom fusion | flops 12288 | bytes 106500 | tf_op jit(solution)/shard_map/scatter-add | solution.py:137
  161.6 2.4 fusion.115
  164.1 5.6 multiply_reduce_fusion.5
  169.7 2.5 fusion.27
  178.6 2.7 collective-permute-done.4
  182.1 6.2 collective-permute-start.6
  188.4 3.6 collective-permute-start.7
  193.0 11.5 %scatter_fusion.1 = f32[12288]{0:T(1024)S(1)} fusion(f32[12288]{0:T(1024)S(1)} %reshape.474, s32[2048]{0:T(1024)S(1)} %broadcast_select_fusion.4, f32[2048]{0:T(1024)S(1)} %broadcast.235), kind=kCustom, calls=%fused_computation.11 | custom fusion | flops 2048 | bytes 32768
  205.2 89.7 %scatter_custom_fusion.1 = f32[3,4096]{0,1:T(8,128)S(1)} fusion(f32[3,4096]{0,1:T(8,128)S(1)} %copy.845, s32[2048]{0:T(1024)} %copy-done.17, f32[]{:T(128)S(6)} %select_n.220, f32[3,4096]{0,1:T(8,128)} %copy.844, s32[2048]{0:T(1024)S(1)} %get-tuple-element.59), kind=kCustom, calls=%fused_computation.24 | custom fusion | flops 12288 | bytes 2154500 | tf_op jit(solution)/shard_map/scatter-add | solution.py:137
  300.2 2.4 fusion.116
  302.6 5.6 multiply_reduce_fusion.4
  308.2 2.5 fusion.28
  322.5 6.5 collective-permute-start.11
  329.0 5.5 collective-permute-start.12
  336.7 11.5 %scatter_fusion.2 = f32[12288]{0:T(1024)S(1)} fusion(f32[12288]{0:T(1024)S(1)} %reshape.478, s32[2048]{0:T(1024)S(1)} %broadcast_select_fusion.4, f32[2048]{0:T(1024)S(1)} %broadcast.236), kind=kCustom, calls=%fused_computation.12 | custom fusion | flops 2048 | bytes 32768
  348.9 89.3 %scatter_custom_fusion.2 = f32[3,4096]{0,1:T(8,128)S(1)} fusion(f32[3,4096]{0,1:T(8,128)S(1)} %copy.871, s32[2048]{0:T(1024)} %copy-done.17, f32[]{:T(128)S(6)} %select_n.220, f32[3,4096]{0,1:T(8,128)} %copy.870, s32[2048]{0:T(1024)S(1)} %get-tuple-element.59), kind=kCustom, calls=%fused_computation.22 | custom fusion | flops 12288 | bytes 2154500 | tf_op jit(solution)/shard_map/scatter-add | solution.py:137
  438.8 2.4 fusion.117
  441.3 5.0 multiply_reduce_fusion.3
  446.4 2.5 fusion.29
  454.7 5.0 collective-permute-done.13
  460.5 7.6 collective-permute-start.15
  468.1 4.5 collective-permute-start.16
  475.1 11.5 %scatter_fusion.3 = f32[12288]{0:T(1024)S(1)} fusion(f32[12288]{0:T(1024)S(1)} %reshape.482, s32[2048]{0:T(1024)S(1)} %broadcast_select_fusion.4, f32[2048]{0:T(1024)S(1)} %broadcast.237), kind=kCustom, calls=%fused_computation.13 | custom fusion | flops 2048 | bytes 32768
  488.6 20.4 %scatter_custom_fusion.3 = f32[3,4096]{0,1:T(8,128)} fusion(f32[3,4096]{0,1:T(8,128)} %copy.896, s32[2048]{0:T(1024)} %copy-done.17, f32[]{:T(128)S(6)} %select_n.220, f32[3,4096]{0,1:T(8,128)S(1)} %copy-done.1, s32[2048]{0:T(1024)S(1)} %get-tuple-element.59), kind=kCustom, calls=%fused_computation.20 | custom fusion | flops 12288 | bytes 106500 | tf_op jit(solution)/shard_map/scatter-add | solution.py:137
  509.1 2.3 copy.918
  513.0 411.6 %all-reduce.20.cloned.1.call-done = f32[2048,128]{1,0:T(8,128)} async-done(((f32[2048,128]{1,0:T(8,128)}), f32[2048,128]{1,0:T(8,128)}) %all-reduce.20.cloned.1.call-update) | async-done | bytes 1048592
  (275 shorter events, 65.4 us)
Async XLA Ops:
  7.2 33.6 %copy-start = (s32[2048]{0:T(1024)S(1)}, s32[2048]{0:T(1024)}, u32[]{:S(2)}) copy-start(s32[2048]{0:T(1024)} %param.19) | copy-start | bytes 24580
  7.2 917.3 %all-reduce.20.cloned.1.call-start = ((), (), s32[]{:S(2)}) async-start(), calls=%async_computation | async-start | bytes 2097152
  17.7 27.6 %collective-permute-start = (f32[2,2,16]{2,1,0:T(2,128)S(1)}, f32[2,2,16]{2,1,0:T(2,128)S(1)}, u32[]{:S(2)}, u32[]{:S(2)}) collective-permute-start(f32[2,2,16]{2,1,0:T(2,128)S(1)} %bitcast.565), channel_id=1, source_target_pairs={{1,0},{2,1},{3,2},{4,3},{5,4},{6,5},{7,6},{9,8},{10,9},{11,10},{12... | collective-permute-start | bytes 776 | tf_op jit(solution)/shard_map/ppermute | solution.py:15
  26.5 19.0 %collective-permute-start.1 = (f32[2,2,128]{2,1,0:T(2,128)S(1)}, f32[2,2,128]{2,1,0:T(2,128)S(1)}, u32[]{:S(2)}, u32[]{:S(2)}) collective-permute-start(f32[2,2,128]{2,1,0:T(2,128)S(1)} %slice_bitcast_fusion.54), channel_id=1, source_target_pairs={{8,0},{16,8},{24,16},{32,24},{40,32},{48,40},{56,48},{64,56},{72,6... | collective-permute-start | bytes 6152 | tf_op jit(solution)/shard_map/ppermute | solution.py:15
  27.8 269.6 %collective-permute-start.8 = (bf16[2,6,2,16,128]{4,3,2,1,0:T(8,128)(2,1)}, bf16[2,6,2,16,128]{4,3,2,1,0:T(8,128)(2,1)}, u32[]{:S(2)}, u32[]{:S(2)}) collective-permute-start(bf16[2,6,2,16,128]{4,3,2,1,0:T(8,128)(2,1)} %bitcast.530), channel_id=1, source_target_pairs={{0,256},{128,384},{1,257},{129,385},{2,258},{130,386},{3,259},{131... | collective-permute-start | bytes 294920 | tf_op jit(solution)/shard_map/ppermute | solution.py:15
  32.3 39.7 %copy-start.17 = (s32[2048]{0:T(1024)}, s32[2048]{0:T(1024)S(1)}, u32[]{:S(2)}) copy-start(s32[2048]{0:T(1024)S(1)} %compare_select_fusion.1) | copy-start | bytes 24580
  32.3 4.0 copy-start.18
  46.1 11.5 %collective-permute-start.2 = (f32[2,2,16]{2,1,0:T(2,128)S(1)}, f32[2,2,16]{2,1,0:T(2,128)S(1)}, u32[]{:S(2)}, u32[]{:S(2)}) collective-permute-start(f32[2,2,16]{2,1,0:T(2,128)S(1)} %bitcast.569), channel_id=1, source_target_pairs={{0,1},{1,2},{2,3},{3,4},{4,5},{5,6},{6,7},{8,9},{9,10},{10,11},{11... | collective-permute-start | bytes 776 | tf_op jit(solution)/shard_map/ppermute | solution.py:15
  53.3 5.0 collective-permute-start.3
  161.6 15.2 %copy-start.15 = (bf16[1,1,2,16,128]{4,3,2,1,0:T(8,128)(2,1)S(1)}, bf16[1,1,2,16,128]{4,3,2,1,0:T(8,128)(2,1)}, u32[]{:S(2)}) copy-start(bf16[1,1,2,16,128]{4,3,2,1,0:T(8,128)(2,1)} %get-tuple-element.35) | copy-start | bytes 24580
  161.6 15.8 %copy-start.14 = (bf16[1,1,2,16,128]{4,3,2,1,0:T(8,128)(2,1)S(1)}, bf16[1,1,2,16,128]{4,3,2,1,0:T(8,128)(2,1)}, u32[]{:S(2)}) copy-start(bf16[1,1,2,16,128]{4,3,2,1,0:T(8,128)(2,1)} %get-tuple-element.132) | copy-start | bytes 24580
  161.6 16.4 %copy-start.16 = (bf16[1,1,2,16,128]{4,3,2,1,0:T(8,128)(2,1)S(1)}, bf16[1,1,2,16,128]{4,3,2,1,0:T(8,128)(2,1)}, u32[]{:S(2)}) copy-start(bf16[1,1,2,16,128]{4,3,2,1,0:T(8,128)(2,1)} %get-tuple-element.39) | copy-start | bytes 24580
  172.5 8.8 collective-permute-start.4
  174.5 7.0 collective-permute-start.5
  182.1 9.9 %collective-permute-start.6 = (f32[2,2,16]{2,1,0:T(2,128)S(1)}, f32[2,2,16]{2,1,0:T(2,128)S(1)}, u32[]{:S(2)}, u32[]{:S(2)}) collective-permute-start(f32[2,2,16]{2,1,0:T(2,128)S(1)} %bitcast.570), channel_id=1, source_target_pairs={{0,1},{1,2},{2,3},{3,4},{4,5},{5,6},{6,7},{8,9},{9,10},{10,11},{11... | collective-permute-start | bytes 776 | tf_op jit(solution)/shard_map/ppermute | solution.py:15
  188.4 4.4 collective-permute-start.7
  312.9 8.8 collective-permute-start.9
  314.9 7.2 collective-permute-start.10
  322.5 12.0 %collective-permute-start.11 = (f32[2,2,16]{2,1,0:T(2,128)S(1)}, f32[2,2,16]{2,1,0:T(2,128)S(1)}, u32[]{:S(2)}, u32[]{:S(2)}) collective-permute-start(f32[2,2,16]{2,1,0:T(2,128)S(1)} %slice_reduce_fusion.1), channel_id=1, source_target_pairs={{0,1},{1,2},{2,3},{3,4},{4,5},{5,6},{6,7},{8,9},{9,10},{10,11},{11... | collective-permute-start | bytes 776 | tf_op jit(solution)/shard_map/ppermute | solution.py:15
  329.0 6.3 collective-permute-start.12
  438.8 10.1 %copy-start.4 = (f32[16,128]{1,0:T(8,128)S(1)}, f32[16,128]{1,0:T(8,128)}, u32[]{:S(2)}) copy-start(f32[16,128]{1,0:T(8,128)} %get-tuple-element.23) | copy-start | bytes 24580
  441.2 13.4 %copy-start.13 = (bf16[1,1,2,16,128]{4,3,2,1,0:T(8,128)(2,1)S(1)}, bf16[1,1,2,16,128]{4,3,2,1,0:T(8,128)(2,1)}, u32[]{:S(2)}) copy-start(bf16[1,1,2,16,128]{4,3,2,1,0:T(8,128)(2,1)} %get-tuple-element.47) | copy-start | bytes 24580
  441.3 13.4 %copy-start.12 = (bf16[1,1,2,16,128]{4,3,2,1,0:T(8,128)(2,1)S(1)}, bf16[1,1,2,16,128]{4,3,2,1,0:T(8,128)(2,1)}, u32[]{:S(2)}) copy-start(bf16[1,1,2,16,128]{4,3,2,1,0:T(8,128)(2,1)} %get-tuple-element.92) | copy-start | bytes 24580
  441.3 13.4 %copy-start.11 = (bf16[1,1,2,16,128]{4,3,2,1,0:T(8,128)(2,1)S(1)}, bf16[1,1,2,16,128]{4,3,2,1,0:T(8,128)(2,1)}, u32[]{:S(2)}) copy-start(bf16[1,1,2,16,128]{4,3,2,1,0:T(8,128)(2,1)} %get-tuple-element.51) | copy-start | bytes 24580
  450.9 8.8 collective-permute-start.13
  453.0 7.0 collective-permute-start.14
  460.5 12.1 %collective-permute-start.15 = (f32[2,2,16]{2,1,0:T(2,128)S(1)}, f32[2,2,16]{2,1,0:T(2,128)S(1)}, u32[]{:S(2)}, u32[]{:S(2)}) collective-permute-start(f32[2,2,16]{2,1,0:T(2,128)S(1)} %slice_reduce_fusion), channel_id=1, source_target_pairs={{0,1},{1,2},{2,3},{3,4},{4,5},{5,6},{6,7},{8,9},{9,10},{10,11},{11... | collective-permute-start | bytes 776 | tf_op jit(solution)/shard_map/ppermute | solution.py:15
  468.1 5.2 collective-permute-start.16
  473.7 38.3 %collective-permute-start.17 = (bf16[2,6,2,16,128]{4,2,1,3,0:T(2,128)(2,1)S(1)}, bf16[2,6,2,16,128]{4,2,1,3,0:T(2,128)(2,1)S(1)}, u32[]{:S(2)}, u32[]{:S(2)}) collective-permute-start(bf16[2,6,2,16,128]{4,2,1,3,0:T(2,128)(2,1)S(1)} %maximum_maximum_fusion), channel_id=1, source_target_pairs={{0,256},{128,384},{1,257},{129,385},{2,258},{130,386},{3,259},{131... | collective-permute-start | bytes 294920 | tf_op jit(solution)/shard_map/ppermute | solution.py:15
  509.0 3.0 copy-start.8
  509.0 3.0 copy-start.9
  509.1 3.0 copy-start.10
  (6 other events, 16.5 us)
Sparse Core Ops, SparseCore 0:
  451.0 473.5 all-reduce.19
where the time goes:
time: 935 us; the launch traced here: 933 us
  waiting for transfers between devices  422 us (45%)
  other arithmetic  385 us (41%)
  starting transfers between devices  68.4 us (7%)
  local copies, waits for them, and re-layouts  38.4 us (4%)
  between operations  17.9 us (2%)
    unnamed x2, waiting for transfers between devices  412 us
    scatter-add x4, other arithmetic, local(): flat_field.at[:, monitor_slots].add(monitor_values, mode='drop')  288 us
    ppermute x18, starting transfers between devices, shifted_2(): return lax.ppermute(block, axis, route)  68.3 us
    unnamed x7, other arithmetic  47.5 us
    reduce_sum x4, other arithmetic, local(): jnp.sum(-(factor * factor / time_step) * contracted, axis=0) * active  21.8 us
  transfers between devices with their start and end apart: 19, of which 8 were waited for; matrix products, arithmetic and copies ran while one was open for 30% of the time, Pallas kernels for 0%

commit v1 on v0

v1 whole, which is shorter than its diff:
```python
import functools

import jax
import jax.numpy as jnp
from jax import lax
from jax.experimental import pallas as pl
from jax.experimental.pallas import tpu as pltpu
from jax.sharding import PartitionSpec as P

MESH = pl.DeviceIdType.MESH
F32 = jnp.float32
BF16 = jnp.bfloat16

NZ = 2
TX = 16
TY = 128
RIM = 4
EX = TX + 2 * RIM
EY = 2 * TY
STEPS = 4
HALF = 2
DT = 0.5
SHARE = 4

AROUND = ((-1, 0), (1, 0), (0, -1), (0, 1), (-1, -1), (-1, 1), (1, -1), (1, 1))


def iota(shape, axis):
    return lax.broadcasted_iota(jnp.int32, shape, axis)


def pack_columns(planes):
    column = iota((TX, TY), 1)
    window = ((column + RIM) // 8) % 16
    packed = planes[0]
    for p in range(1, len(planes)):
        packed = jnp.where(window == p, pltpu.roll(planes[p], 8 * p, 1), packed)
    return packed


def pack_rows(one, two):
    low = iota((8, TY), 0) < RIM
    first = jnp.where(low, one[:8], one[8:])
    second = pltpu.roll(jnp.where(low, two[:8], two[8:]), RIM, 0)
    return jnp.where(low, first, second), jnp.where(low, second, first)


def unpack_rows(after, before):
    low = iota((8, TY), 0) < RIM
    return jnp.where(low, after, before), pltpu.roll(jnp.where(low, before, after), RIM, 0)


def merge_columns(right, left, corners):
    side = iota((TX, TY), 1) % 8 < RIM
    beside = jnp.where(side, right, left)
    side = side[:8]
    from_after_right, from_after_left, from_before_right, from_before_left = corners
    low = iota((8, TY), 0) < RIM
    after = jnp.where(side, from_after_right, from_after_left)
    before = jnp.where(side, from_before_right, from_before_left)
    return jnp.concatenate([beside, jnp.where(low, after, before)], axis=0)


def extended(tile, rows, columns, p):
    body = jnp.concatenate([tile, rows], axis=0)
    beside = columns if p == 0 else pltpu.roll(columns, TY - 8 * p, 1)
    return jnp.concatenate([body, beside], axis=1)


def next_x(v):
    return pltpu.roll(v, EX - 1, 0) - v


def next_y(v):
    return pltpu.roll(v, EY - 1, 1) - v


def next_z(v):
    return [v[1] - v[0], -v[1]]


def last_x(v):
    return v - pltpu.roll(v, 1, 0)


def last_y(v):
    return v - pltpu.roll(v, 1, 1)


def last_z(v):
    return [v[0], v[1] - v[0]]


def curl(v, along_x, along_y, along_z):
    z_of_y, z_of_x = along_z(v[1]), along_z(v[0])
    return (
        [along_y(v[2][z]) - z_of_y[z] for z in range(NZ)],
        [z_of_x[z] - along_x(v[2][z]) for z in range(NZ)],
        [along_x(v[1][z]) - along_y(v[0][z]) for z in range(NZ)],
    )


def curl_up(v):
    return curl(v, next_x, next_y, next_z)


def curl_down(v):
    return curl(v, last_x, last_y, last_z)


def kernel(
    n_gx,
    n_gy,
    fields,
    stored,
    material,
    design,
    mat_eps,
    mat_chi,
    source_wave,
    source_cells,
    monitor_cells,
    owners,
    fields_next,
    stored_next,
    design_grad,
    col_out,
    colh_out,
    row_out,
    rowh_out,
    col_in,
    corner_in,
    row_in,
    colh_in,
    rowh_in,
    half_in,
    records,
    state,
    counts_ref,
    chosen,
    tiles,
    shares,
    gathered,
    own_sem,
    ownh_sem,
    half_send,
    in_sem,
    inh_sem,
    half_sem,
    record_send,
    record_sem,
    tile_send,
    tile_sem,
    share_send,
    share_sem,
    local_sem,
):
    grp, gx, gy = lax.axis_index("grp"), lax.axis_index("gx"), lax.axis_index("gy")
    forward = grp < 2
    ahead = jnp.where(forward, 1, 0)
    half_lane = grp + 2 * ahead
    twin = jnp.where(forward, grp + 2, grp - 2)

    def device(lane, dx, dy):
        return {
            "grp": lane,
            "gx": lax.rem(gx + dx + n_gx, n_gx),
            "gy": lax.rem(gy + dy + n_gy, n_gy),
        }

    barrier = pltpu.get_barrier_semaphore()

    def greet(target):
        pl.semaphore_signal(barrier, inc=1, device_id=target, device_id_type=MESH)

    for dx, dy in AROUND:
        greet(device(grp, dx, dy))
        greet(device(twin, dx, dy))
    greet(device(twin, 0, 0))

    @pl.when(forward)
    def _():
        def column(i, carry):
            greet({"grp": 2 + i // n_gy, "gx": gx, "gy": lax.rem(i, n_gy)})
            return carry

        lax.fori_loop(0, 2 * n_gy, column, 0)

    @pl.when(jnp.logical_not(forward))
    def _():
        def line(j, carry):
            greet(device(grp, j, 0))
            return carry

        lax.fori_loop(1, n_gx, line, 0)

        def column(i, carry):
            greet(device(lax.rem(grp + i // n_gy, 4), 0, lax.rem(i, n_gy)))
            return carry

        lax.fori_loop(1, 4 * n_gy, column, 0)

    def lookup(index, entries):
        value = jnp.zeros(index.shape, F32)
        for k in range(4):
            value = jnp.where(index == k, entries[k], value)
        return value

    kinds = [material[z] for z in range(NZ)]
    eps = [lookup(kinds[z], mat_eps) + design[...] for z in range(NZ)]
    chi = [lookup(kinds[z], mat_chi) for z in range(NZ)]
    own = [fields[c, z] for c in range(6) for z in range(NZ)] + eps + chi
    col_out[...] = pack_columns(own)
    for i in range(8):
        row_out[0, i], row_out[1, i] = pack_rows(own[2 * i], own[2 * i + 1])

    pl.semaphore_wait(barrier, jnp.where(forward, 17 + 2 * n_gy, 17 + n_gx - 1 + 4 * n_gy - 1))

    def row_copy(i):
        return pltpu.make_async_remote_copy(
            src_ref=row_out.at[i],
            dst_ref=row_in.at[i],
            send_sem=own_sem.at[i],
            recv_sem=in_sem.at[i],
            device_id=device(grp, *AROUND[i]),
            device_id_type=MESH,
        )

    def col_copy(i):
        return pltpu.make_async_remote_copy(
            src_ref=col_out,
            dst_ref=col_in.at[i - 2],
            send_sem=own_sem.at[i],
            recv_sem=in_sem.at[i],
            device_id=device(grp, *AROUND[i]),
            device_id_type=MESH,
        )

    def corner_copy(i):
        start = 0 if AROUND[i][0] < 0 else 8
        return pltpu.make_async_remote_copy(
            src_ref=col_out.at[pl.ds(start, 8)],
            dst_ref=corner_in.at[i - 4],
            send_sem=own_sem.at[i],
            recv_sem=in_sem.at[i],
            device_id=device(grp, *AROUND[i]),
            device_id_type=MESH,
        )

    def rim_copies():
        return [row_copy(0), row_copy(1), col_copy(2), col_copy(3)] + [corner_copy(i) for i in range(4, 8)]

    for copy in rim_copies():
        copy.start()

    for k in range(HALF):
        planes = [stored[k, c, z].astype(F32) for c in range(6) for z in range(NZ)]
        colh_out[k] = pack_columns(planes).astype(BF16)
        for i in range(3):
            one = pack_rows(planes[4 * i], planes[4 * i + 1])
            two = pack_rows(planes[4 * i + 2], planes[4 * i + 3])
            for side in range(2):
                rowh_out[side, 3 * k + i] = jnp.concatenate([one[side], two[side]], axis=0).astype(BF16)

    def half_copy(which, i):
        if i < 2:
            src, dst = rowh_out.at[i], rowh_in.at[which, i]
        else:
            src, dst = colh_out, colh_in.at[which, i - 2]
        return pltpu.make_async_remote_copy(
            src_ref=src,
            dst_ref=dst,
            send_sem=ownh_sem.at[i],
            recv_sem=inh_sem.at[which, i],
            device_id=device(half_lane, *AROUND[i]),
            device_id_type=MESH,
        )

    for i in range(8):
        half_copy(ahead, i).start()

    def whole_half():
        return pltpu.make_async_remote_copy(
            src_ref=stored,
            dst_ref=half_in,
            send_sem=half_send,
            recv_sem=half_sem,
            device_id=device(half_lane, 0, 0),
            device_id_type=MESH,
        )

    @pl.when(forward)
    def _():
        whole_half().start()

    row = iota((NZ * EX, TY), 0)
    depth = jnp.where(row >= EX, 1, 0)
    row = row - depth * EX
    x = gx * TX + jnp.where(row < TX + RIM, row, row - EX)
    sought_x = jnp.where((x >= 0) & (x < n_gx * TX), depth * (n_gx * TX) + x, -1)
    column = iota((TY, TY), 0)
    sought_y = gy * TY + column
    sought_high = sought_y[:8] + TY
    sought_low = sought_y[TY - 8 :] - TY
    listed = jnp.where(forward, source_cells[...], monitor_cells[...])
    listed_x = listed // (n_gy * TY)
    listed_y = listed % (n_gy * TY)

    def hits(found):
        return jnp.where(found, 1.0, 0.0)

    def wide(m, i, rows):
        return jnp.broadcast_to(m[i : i + 1], (rows, TY))

    entries = listed.shape[0]
    rows_hit = jnp.concatenate(
        [hits(wide(listed_x, i, NZ * EX) == sought_x) for i in range(entries)], axis=1
    ).astype(BF16)
    columns_hit = jnp.concatenate(
        [hits(wide(listed_y, i, TY) == sought_y) for i in range(entries)], axis=1
    ).astype(BF16)
    high_hit = jnp.concatenate([hits(wide(listed_y, i, 8) == sought_high) for i in range(entries)], axis=1)
    low_hit = jnp.concatenate([hits(wide(listed_y, i, 8) == sought_low) for i in range(entries)], axis=1)
    rim_hit = jnp.concatenate(
        [high_hit, jnp.zeros((TY - 16, entries * TY), F32), low_hit], axis=0
    ).astype(BF16)

    def tally(a, b):
        return lax.dot_general(a, b, (((1,), (1,)), ((), ())), preferred_element_type=F32)

    counts_ref[...] = jnp.concatenate([tally(rows_hit, columns_hit), tally(rows_hit, rim_hit)], axis=1)

    @pl.when(jnp.logical_not(forward))
    def _():
        lanes = owners.shape[1]
        pick = iota((TX, lanes), 1) == iota((TX, lanes), 0) * n_gy + gy
        coarse, fine = [], []
        for j in range(n_gx):
            line = jnp.broadcast_to(owners[pl.ds(lax.rem(gx - j + n_gx, n_gx), 1)], (TX, lanes))
            line = jnp.where(pick, line, 0)
            part = line // 64 * 64
            coarse.append(part.astype(F32))
            fine.append((line - part).astype(F32))
        rows = 4 * n_gy * SHARE
        ones = jnp.ones((rows, lanes), BF16)
        owner = tally(ones, jnp.concatenate(coarse, axis=0).astype(BF16))
        owner = owner + tally(ones, jnp.concatenate(fine, axis=0).astype(BF16))
        place = iota((rows, n_gx * TX), 0)
        share = place // SHARE
        lane = (grp + share // n_gy) % 4
        spot = (gy + share % n_gy) % n_gy
        wanted = ((lane * n_gx + gx) * n_gy + spot) * SHARE + place % SHARE
        chosen[...] = jnp.where(owner == wanted.astype(F32), 1.0, 0.0).astype(BF16)

    row = iota((EX, EY), 0)
    column = iota((EX, EY), 1)
    x = gx * TX + jnp.where(row < TX + RIM, row, row - EX)
    y = gy * TY + jnp.where(column < TY + TY // 2, column, column - EY)
    inside = (x >= 0) & (x < n_gx * TX) & (y >= 0) & (y < n_gy * TY)
    unit = jnp.where(inside, 1.0, 0.0)
    step = jnp.where(inside, DT, 0.0)
    counts = [counts_ref[z * EX : (z + 1) * EX] for z in range(NZ)]

    for copy in rim_copies():
        copy.wait_recv()
    columns = merge_columns(col_in[0], col_in[1], [corner_in[i] for i in range(4)])
    whole = []
    for i in range(8):
        for k, rows in enumerate(unpack_rows(row_in[0, i], row_in[1, i])):
            whole.append(extended(own[2 * i + k], rows, columns, 2 * i + k))
    eps = whole[12:14]
    chi = whole[14:16]
    whole = [jnp.where(inside, v, 0.0) for v in whole[:12]]
    first = [whole[2 * c : 2 * c + 2] for c in range(3)]
    second = [whole[2 * c : 2 * c + 2] for c in range(3, 6)]

    def state_copy():
        return pltpu.make_async_copy(state, fields_next, local_sem.at[0])

    def finish(electric, magnetic):
        for c in range(3):
            for z in range(NZ):
                state[c, z] = electric[c][z][:TX, :TY]
                state[3 + c, z] = magnetic[c][z][:TX, :TY]
        state_copy().start()

    def record_copy(n):
        return pltpu.make_async_remote_copy(
            src_ref=records.at[n],
            dst_ref=stored_next.at[n - HALF],
            send_sem=record_send.at[n - HALF],
            recv_sem=record_sem.at[n - HALF],
            device_id=device(half_lane, 0, 0),
            device_id_type=MESH,
        )

    def kept_copy(n):
        return pltpu.make_async_copy(records.at[n], stored_next.at[n], local_sem.at[1 + n])

    def square(v, z):
        return v[0][z] * v[0][z] + v[1][z] * v[1][z] + v[2][z] * v[2][z]

    @pl.when(forward)
    def _():
        electric, magnetic = first, second
        for n in range(STEPS):
            factor = [step / (eps[z] + chi[z] * square(electric, z)) for z in range(NZ)]
            turn = curl_up(electric)
            magnetic = [[magnetic[c][z] - step * turn[c][z] for z in range(NZ)] for c in range(3)]
            turn = curl_down(magnetic)
            for c in range(3):
                for z in range(NZ):
                    records[n, c, z] = electric[c][z][:TX, :TY].astype(BF16)
                    records[n, 3 + c, z] = turn[c][z][:TX, :TY].astype(BF16)
            (kept_copy if n < HALF else record_copy)(n).start()
            wave = source_wave[lax.rem(grp, 2), n]
            electric = [[electric[c][z] + factor[z] * turn[c][z] for z in range(NZ)] for c in range(3)]
            electric[0] = [electric[0][z] + wave * counts[z] for z in range(NZ)]
        finish(electric, magnetic)

    def rims_of_half(which, k):
        rows = []
        for i in range(3):
            after = rowh_in[which, 0, 3 * k + i].astype(F32)
            before = rowh_in[which, 1, 3 * k + i].astype(F32)
            rows.extend(unpack_rows(after[:8], before[:8]))
            rows.extend(unpack_rows(after[8:], before[8:]))
        packed = [colh_in[which, i, k].astype(F32) for i in range(6)]
        corners = [packed[2][:8], packed[3][:8], packed[4][8:], packed[5][8:]]
        return rows, merge_columns(packed[0], packed[1], corners)

    def snapshot(which, k):
        tile = stored if which == 0 else half_in
        rows, columns = rims_of_half(which, k)
        planes = [
            extended(tile[k, c, z].astype(F32), rows[2 * c + z], columns, 2 * c + z)
            for c in range(6)
            for z in range(NZ)
        ]
        past = [planes[2 * c : 2 * c + 2] for c in range(3)]
        curled = [planes[2 * c : 2 * c + 2] for c in range(3, 6)]
        return past, curled

    @pl.when(jnp.logical_not(forward))
    def _():
        electric, magnetic = first, second
        gradient = jnp.zeros((TX, TY), F32)
        for n in range(STEPS - 1, -1, -1):
            which, k = (0, n - HALF) if n >= HALF else (1, n)
            if k == HALF - 1:
                for i in range(8):
                    half_copy(which, i).wait_recv()
                if which == 1:
                    whole_half().wait_recv()
            past, curled = snapshot(which, k)
            factor = [DT / (eps[z] + chi[z] * square(past, z)) for z in range(NZ)]
            inner = [
                curled[0][z] * electric[0][z] + curled[1][z] * electric[1][z] + curled[2][z] * electric[2][z]
                for z in range(NZ)
            ]
            turn = curl_up([[factor[z] * electric[c][z] for z in range(NZ)] for c in range(3)])
            magnetic = [[magnetic[c][z] + unit * turn[c][z] for z in range(NZ)] for c in range(3)]
            turn = curl_down(magnetic)
            slope = [factor[z] * factor[z] * inner[z] for z in range(NZ)]
            gradient = gradient - (1.0 / DT) * (slope[0] + slope[1])[:TX, :TY]
            weight = [counts[z] - (2.0 / DT) * chi[z] * slope[z] for z in range(NZ)]
            electric = [
                [electric[c][z] + weight[z] * past[c][z] - step * turn[c][z] for z in range(NZ)] for c in range(3)
            ]
        tiles[0] = gradient
        finish(electric, magnetic)

    def tile_copy(j):
        return pltpu.make_async_remote_copy(
            src_ref=tiles.at[0],
            dst_ref=tiles.at[j],
            send_sem=tile_send.at[j],
            recv_sem=tile_sem.at[j],
            device_id=device(grp, j, 0),
            device_id_type=MESH,
        )

    def share_copy(i):
        return pltpu.make_async_remote_copy(
            src_ref=shares.at[i],
            dst_ref=gathered.at[i],
            send_sem=share_send.at[i],
            recv_sem=share_sem.at[i],
            device_id=device(lax.rem(grp + i // n_gy, 4), 0, lax.rem(i, n_gy)),
            device_id_type=MESH,
        )

    def each(low, high, act):
        def body(i, carry):
            act(i)
            return carry

        lax.fori_loop(low, high, body, 0)

    @pl.when(jnp.logical_not(forward))
    def _():
        each(1, n_gx, lambda j: tile_copy(j).start())
        each(1, n_gx, lambda j: tile_copy(j).wait_recv())
        rest = jnp.concatenate([tiles[j] for j in range(n_gx)], axis=0)
        total = jnp.zeros((4 * n_gy * SHARE, TY), F32)
        for _ in range(3):
            part = rest.astype(BF16)
            total = total + jnp.dot(chosen[...], part, preferred_element_type=F32)
            rest = rest - part.astype(F32)
        for i in range(4 * n_gy):
            shares[i] = total[SHARE * i : SHARE * (i + 1)]
        gathered[0] = total[:SHARE]
        each(1, 4 * n_gy, lambda i: share_copy(i).start())

    sum_of = jnp.zeros((SHARE, TY), F32)
    for lane in (2, 3):
        start = lax.rem(grp + 4 - lane, 4) * n_gy
        each(start + jnp.where(start == 0, 1, 0), start + n_gy, lambda i: share_copy(i).wait_recv())
        for j in range(n_gy):
            sum_of = sum_of + gathered[start + j]
    design_grad[...] = sum_of

    for copy in rim_copies():
        copy.wait_send()
    for i in range(8):
        half_copy(ahead, i).wait_send()
    state_copy().wait()

    @pl.when(forward)
    def _():
        whole_half().wait_send()
        for n in range(STEPS):
            if n < HALF:
                kept_copy(n).wait()
            else:
                record_copy(n).wait_send()

    @pl.when(jnp.logical_not(forward))
    def _():
        for n in range(HALF, STEPS):
            record_copy(n).wait_recv()
        each(1, n_gx, lambda j: tile_copy(j).wait_send())
        each(1, 4 * n_gy, lambda i: share_copy(i).wait_send())


def local(fields, stored, material, design, mat_eps, mat_chi, source_wave, source_cells, monitor_cells, owners):
    n_gx, n_gy = lax.axis_size("gx"), lax.axis_size("gy")
    vmem = pl.BlockSpec(memory_space=pltpu.VMEM)
    smem = pl.BlockSpec(memory_space=pltpu.SMEM)
    anywhere = pl.BlockSpec(memory_space=pl.ANY)
    dma = pltpu.SemaphoreType.DMA
    cells = source_cells.shape[0]
    fields_next, stored_next, design_grad = pl.pallas_call(
        functools.partial(kernel, n_gx, n_gy),
        out_shape=(
            jax.ShapeDtypeStruct((6, NZ, TX, TY), F32),
            jax.ShapeDtypeStruct((HALF, 6, NZ, TX, TY), BF16),
            jax.ShapeDtypeStruct((SHARE, TY), F32),
        ),
        in_specs=[vmem, vmem, vmem, vmem, smem, smem, smem, vmem, vmem, vmem],
        out_specs=(anywhere, anywhere, vmem),
        scratch_shapes=[
            pltpu.VMEM((TX, TY), F32),
            pltpu.VMEM((HALF, TX, TY), BF16),
            pltpu.VMEM((2, 8, 8, TY), F32),
            pltpu.VMEM((2, 6, TX, TY), BF16),
            pltpu.VMEM((2, TX, TY), F32),
            pltpu.VMEM((4, 8, TY), F32),
            pltpu.VMEM((2, 8, 8, TY), F32),
            pltpu.VMEM((2, 6, HALF, TX, TY), BF16),
            pltpu.VMEM((2, 2, 6, TX, TY), BF16),
            pltpu.VMEM((HALF, 6, NZ, TX, TY), BF16),
            pltpu.VMEM((STEPS, 6, NZ, TX, TY), BF16),
            pltpu.VMEM((6, NZ, TX, TY), F32),
            pltpu.VMEM((NZ * EX, EY), F32),
            pltpu.VMEM((4 * n_gy * SHARE, n_gx * TX), BF16),
            pltpu.VMEM((n_gx, TX, TY), F32),
            pltpu.VMEM((4 * n_gy, SHARE, TY), F32),
            pltpu.VMEM((4 * n_gy, SHARE, TY), F32),
            dma((8,)),
            dma((8,)),
            dma,
            dma((8,)),
            dma((2, 8)),
            dma,
            dma((HALF,)),
            dma((HALF,)),
            dma((n_gx,)),
            dma((n_gx,)),
            dma((4 * n_gy,)),
            dma((4 * n_gy,)),
            dma((3,)),
        ],
        compiler_params=pltpu.CompilerParams(
            collective_id=0, has_side_effects=True, vmem_limit_bytes=32 * 1024 * 1024
        ),
        name="interval",
    )(
        fields[0],
        stored[0],
        material,
        design,
        mat_eps,
        mat_chi,
        source_wave,
        source_cells.reshape(cells // TY, TY),
        monitor_cells.reshape(cells // TY, TY),
        owners.reshape(n_gx, TX * n_gy),
    )
    return fields_next[None], stored_next[None], design_grad


def solution(mesh):
    in_specs = (
        P("grp", None, None, "gx", "gy"),
        P("grp", None, None, None, "gx", "gy"),
        P(None, "gx", "gy"),
        P("gx", "gy"),
        P(),
        P(),
        P(),
        P(),
        P(),
        P(),
    )
    out_specs = (
        P("grp", None, None, "gx", "gy"),
        P("grp", None, None, None, "gx", "gy"),
        P(("grp", "gx", "gy"), None),
    )
    return jax.shard_map(local, mesh=mesh, in_specs=in_specs, out_specs=out_specs, check_vma=False)
```

time: 935 us -> 57.3 us (0.06)
  waiting for transfers between devices: 422 us -> 0 us
  other arithmetic: 385 us -> 0 us
  starting transfers between devices: 68.4 us -> 0 us
  Pallas kernels: 0 us -> 47.7 us
  local copies, waits for them, and re-layouts: 38.4 us -> 8.44 us
  between operations: 17.9 us -> 0.67 us
    unnamed x2 -> x0, waiting for transfers between devices: 412 us -> none
    scatter-add x4 -> x0, other arithmetic: 288 us -> none  [local(): flat_field.at[:, monitor_slots].add(monitor_values, mode='drop')]
    ppermute x18 -> x0, starting transfers between devices: 68.3 us -> none  [shifted_2(): return lax.ppermute(block, axis, route)]
    pallas_call x0 -> x1, Pallas kernels: none -> 47.7 us  [local(): pl.pallas_call(functools.partial(kernel, n_gx, n_gy), out_shape=(jax.Shap...]
    unnamed x7 -> x0, other arithmetic: 47.5 us -> none
    reduce_sum x8 -> x0, other arithmetic: 22 us -> none  [the longest x4 21.8 us: local(): jnp.sum(-(factor * factor / time_step) * contracted, axis=0) * active]
    convert_element_type x11 -> x0, local copies, waits for them, and re-layouts: 14 us -> none  [the longest x8 7.99 us: local(): past_field = snapshot[:3].astype(jnp.float32)]
    ppermute x18 -> x0, waiting for transfers between devices: 10.8 us -> none  [shifted_2(): return lax.ppermute(block, axis, route)]
  transfers between devices with their start and end apart: 19 -> 0, of which waited for: 8 -> 0; matrix products, arithmetic and copies ran while one was open for 30% -> 0% of each run, Pallas kernels for 0% -> 0%
where the time goes in v1:
time: 57.3 us; the launch traced here: 56.8 us
  Pallas kernels  47.7 us (83%)
  local copies, waits for them, and re-layouts  8.44 us (15%)
  between operations  0.67 us (1%)
    pallas_call x1, Pallas kernels, local(): pl.pallas_call(functools.partial(kernel, n_gx, n_gy), out_shape=(jax.Shap...  47.7 us
    unnamed x23, local copies, waits for them, and re-layouts  8.44 us

profile of v1, /device:TPU:1, one launch (start us, length us, event | category | flops | bytes accessed | tf_op | source)
XLA Modules:
  0.0 56.8 jit_solution(5815763675780567205)
XLA Ops:
  0.6 0.0 copy-start.3
  0.6 0.0 copy-start.7
  0.7 0.7 %copy-done.3 = f32[16,128]{1,0:T(8,128)S(1)} copy-done((f32[16,128]{1,0:T(8,128)S(1)}, f32[16,128]{1,0:T(8,128)}, u32[]{:S(2)}) %copy-start.3) | copy-done | bytes 8216
  1.3 0.0 copy-done.7
  1.3 0.0 copy-start
  1.3 0.9 %copy-done = f32[1,6,2,16,128]{4,3,2,1,0:T(8,128)S(1)} copy-done((f32[1,6,2,16,128]{4,3,2,1,0:T(8,128)S(1)}, f32[1,6,2,16,128]{4,3,2,1,0:T(8,128)}, u32[]{:S(2)}) %copy-start) | copy-done | bytes 98328
  2.2 0.0 copy-start.1
  2.2 0.9 %copy-done.1 = bf16[1,2,6,2,16,128]{5,4,3,2,1,0:T(8,128)(2,1)S(1)} copy-done((bf16[1,2,6,2,16,128]{5,4,3,2,1,0:T(8,128)(2,1)S(1)}, bf16[1,2,6,2,16,128]{5,4,3,2,1,0:T(8,128)(2,1)}, u32[]{:S(2)}) %copy-start.1) | copy-done | bytes 98328
  3.1 0.0 copy-start.2
  3.1 0.7 %copy-done.2 = s32[2,16,128]{2,1,0:T(8,128)S(1)} copy-done((s32[2,16,128]{2,1,0:T(8,128)S(1)}, s32[2,16,128]{2,1,0:T(8,128)}, u32[]{:S(2)}) %copy-start.2) | copy-done | bytes 16408
  3.8 0.0 copy-start.4
  3.8 0.7 %copy-done.4 = s32[2048]{0:T(1024)S(1)} copy-done((s32[2048]{0:T(1024)S(1)}, s32[2048]{0:T(1024)}, u32[]{:S(2)}) %copy-start.4) | copy-done | bytes 8216
  4.5 0.0 copy-start.5
  4.5 0.7 %copy-done.5 = s32[2048]{0:T(1024)S(1)} copy-done((s32[2048]{0:T(1024)S(1)}, s32[2048]{0:T(1024)}, u32[]{:S(2)}) %copy-start.5) | copy-done | bytes 8216
  5.2 0.0 copy-start.6
  5.2 0.7 %copy-done.6 = s32[2048]{0:T(1024)S(1)} copy-done((s32[2048]{0:T(1024)S(1)}, s32[2048]{0:T(1024)}, u32[]{:S(2)}) %copy-start.6) | copy-done | bytes 8216
  5.9 0.0 copy-start.8
  5.9 0.7 %copy-done.8 = f32[4]{0:T(128)S(1)} copy-done((f32[4]{0:T(128)S(1)}, f32[4]{0:T(128)}, u32[]{:S(2)}) %copy-start.8) | copy-done | bytes 40
  6.6 0.0 copy-start.9
  6.6 0.7 %copy-done.9 = f32[4]{0:T(128)S(1)} copy-done((f32[4]{0:T(128)S(1)}, f32[4]{0:T(128)}, u32[]{:S(2)}) %copy-start.9) | copy-done | bytes 40
  7.2 47.7 %interval.1 = (f32[6,2,16,128]{3,2,1,0:T(8,128)S(1)}, bf16[2,6,2,16,128]{4,3,2,1,0:T(8,128)(2,1)S(1)}, f32[4,128]{1,0:T(4,128)S(1)}) custom-call(f32[6,2,16,128]{3,2,1,0:T(8,128)S(1)} %bitcast.9, bf16[2,6,2,16,128]{4,3,2,1,0:T(8,128)(2,1)S(1)} %bitcast.10, s32[2,16,128]{2,1,0:T(8,128)S(1)} %copy-done.2, f32[16,128]{1,0:T(8,128)S(1)} %copy-done.3, ...), custom_call_target="tpu_custom_call" | custom-call | tf_op jit(solution)/shard_map/interval/pallas_call | solution.py:553
  55.0 0.6 %copy.16 = f32[1,6,2,16,128]{4,3,2,1,0:T(8,128)} copy(f32[1,6,2,16,128]{4,3,2,1,0:T(8,128)S(1)} %bitcast.8) | data formatting | bytes 196608
  55.6 0.6 %copy.17 = bf16[1,2,6,2,16,128]{5,4,3,2,1,0:T(8,128)(2,1)} copy(bf16[1,2,6,2,16,128]{5,4,3,2,1,0:T(8,128)(2,1)S(1)} %bitcast.7) | data formatting | bytes 196608
  56.2 0.6 %copy.18 = f32[4,128]{1,0:T(4,128)} copy(f32[4,128]{1,0:T(4,128)S(1)} %get-tuple-element.14) | data formatting | bytes 4096
Async XLA Ops:
  0.6 0.7 %copy-start.3 = (f32[16,128]{1,0:T(8,128)S(1)}, f32[16,128]{1,0:T(8,128)}, u32[]{:S(2)}) copy-start(f32[16,128]{1,0:T(8,128)} %design.1) | copy-start | bytes 24580
  0.6 0.7 %copy-start.7 = (f32[2,4]{1,0:T(2,128)S(1)}, f32[2,4]{1,0:T(2,128)}, u32[]{:S(2)}) copy-start(f32[2,4]{1,0:T(2,128)} %source_wave.1) | copy-start | bytes 100
  1.3 0.9 %copy-start = (f32[1,6,2,16,128]{4,3,2,1,0:T(8,128)S(1)}, f32[1,6,2,16,128]{4,3,2,1,0:T(8,128)}, u32[]{:S(2)}) copy-start(f32[1,6,2,16,128]{4,3,2,1,0:T(8,128)} %param.10) | copy-start | bytes 294916
  2.2 0.9 %copy-start.1 = (bf16[1,2,6,2,16,128]{5,4,3,2,1,0:T(8,128)(2,1)S(1)}, bf16[1,2,6,2,16,128]{5,4,3,2,1,0:T(8,128)(2,1)}, u32[]{:S(2)}) copy-start(bf16[1,2,6,2,16,128]{5,4,3,2,1,0:T(8,128)(2,1)} %param.11) | copy-start | bytes 294916
  3.1 0.7 %copy-start.2 = (s32[2,16,128]{2,1,0:T(8,128)S(1)}, s32[2,16,128]{2,1,0:T(8,128)}, u32[]{:S(2)}) copy-start(s32[2,16,128]{2,1,0:T(8,128)} %material.1) | copy-start | bytes 49156
  3.8 0.7 %copy-start.4 = (s32[2048]{0:T(1024)S(1)}, s32[2048]{0:T(1024)}, u32[]{:S(2)}) copy-start(s32[2048]{0:T(1024)} %param.17) | copy-start | bytes 24580
  4.5 0.7 %copy-start.5 = (s32[2048]{0:T(1024)S(1)}, s32[2048]{0:T(1024)}, u32[]{:S(2)}) copy-start(s32[2048]{0:T(1024)} %param.18) | copy-start | bytes 24580
  5.2 0.7 %copy-start.6 = (s32[2048]{0:T(1024)S(1)}, s32[2048]{0:T(1024)}, u32[]{:S(2)}) copy-start(s32[2048]{0:T(1024)} %param.19) | copy-start | bytes 24580
  5.9 0.7 %copy-start.8 = (f32[4]{0:T(128)S(1)}, f32[4]{0:T(128)}, u32[]{:S(2)}) copy-start(f32[4]{0:T(128)} %mat_eps.1) | copy-start | bytes 52
  6.6 0.7 %copy-start.9 = (f32[4]{0:T(128)S(1)}, f32[4]{0:T(128)}, u32[]{:S(2)}) copy-start(f32[4]{0:T(128)} %mat_chi.1) | copy-start | bytes 52

commit v2 on v1

--- a/solution.py
+++ b/solution.py
@@ -25,16 +25,20 @@
 AROUND = ((-1, 0), (1, 0), (0, -1), (0, 1), (-1, -1), (-1, 1), (1, -1), (1, 1))
 
 
+def far_first(length):
+    return sorted(range(length), key=lambda j: -min(j, length - j))
+
+
 def iota(shape, axis):
     return lax.broadcasted_iota(jnp.int32, shape, axis)
 
 
-def pack_columns(planes):
+def pack_columns(planes, slot=8):
     column = iota((TX, TY), 1)
-    window = ((column + RIM) // 8) % 16
+    window = ((column + slot // 2) // slot) % (TY // slot)
     packed = planes[0]
     for p in range(1, len(planes)):
-        packed = jnp.where(window == p, pltpu.roll(planes[p], 8 * p, 1), packed)
+        packed = jnp.where(window == p, pltpu.roll(planes[p], slot * p, 1), packed)
     return packed
 
 
@@ -50,8 +54,24 @@
     return jnp.where(low, after, before), pltpu.roll(jnp.where(low, before, after), RIM, 0)
 
 
-def merge_columns(right, left, corners):
-    side = iota((TX, TY), 1) % 8 < RIM
+def pack_thin_rows(planes):
+    row = iota((8, TY), 0)
+    both = [jnp.where(row < RIM, p[:8], p[8:]) for p in planes]
+    before = after = both[0]
+    for q in range(1, len(planes)):
+        turned = pltpu.roll(both[q], 2 * q, 0)
+        before = jnp.where(row // 2 == q, turned, before)
+        after = jnp.where((row // 2 + 1) % 4 == q, turned, after)
+    return before, after
+
+
+def unpack_thin_rows(after, before, q):
+    rows = jnp.where(iota((8, TY), 0) // 2 == q, after, before)
+    return rows if q == 0 else pltpu.roll(rows, 8 - 2 * q, 0)
+
+
+def merge_columns(right, left, corners, slot=8):
+    side = iota((TX, TY), 1) % slot < slot // 2
     beside = jnp.where(side, right, left)
     side = side[:8]
     from_after_right, from_after_left, from_before_right, from_before_left = corners
@@ -61,9 +81,9 @@
     return jnp.concatenate([beside, jnp.where(low, after, before)], axis=0)
 
 
-def extended(tile, rows, columns, p):
+def extended(tile, rows, columns, shift):
     body = jnp.concatenate([tile, rows], axis=0)
-    beside = columns if p == 0 else pltpu.roll(columns, TY - 8 * p, 1)
+    beside = columns if shift == 0 else pltpu.roll(columns, TY - shift, 1)
     return jnp.concatenate([body, beside], axis=1)
 
 
@@ -111,6 +131,19 @@
 def kernel(
     n_gx,
     n_gy,
+    fields_in,
+    stored_in,
+    material_in,
+    design_in,
+    mat_eps_in,
+    mat_chi_in,
+    source_wave_in,
+    source_cells_in,
+    monitor_cells_in,
+    owners_in,
+    fields_next,
+    stored_next,
+    design_grad,
     fields,
     stored,
     material,
@@ -121,9 +154,6 @@
     source_cells,
     monitor_cells,
     owners,
-    fields_next,
-    stored_next,
-    design_grad,
     col_out,
     colh_out,
     row_out,
@@ -134,6 +164,10 @@
     colh_in,
     rowh_in,
     half_in,
+    rowc_out,
+    rowc_in,
+    colc_out,
+    colc_in,
     records,
     state,
     counts_ref,
@@ -147,6 +181,8 @@
     in_sem,
     inh_sem,
     half_sem,
+    thin_send,
+    thin_sem,
     record_send,
     record_sem,
     tile_send,
@@ -154,11 +190,10 @@
     share_send,
     share_sem,
     local_sem,
+    load_sem,
 ):
     grp, gx, gy = lax.axis_index("grp"), lax.axis_index("gx"), lax.axis_index("gy")
     forward = grp < 2
-    ahead = jnp.where(forward, 1, 0)
-    half_lane = grp + 2 * ahead
     twin = jnp.where(forward, grp + 2, grp - 2)
 
     def device(lane, dx, dy):
@@ -173,32 +208,69 @@
     def greet(target):
         pl.semaphore_signal(barrier, inc=1, device_id=target, device_id_type=MESH)
 
-    for dx, dy in AROUND:
-        greet(device(grp, dx, dy))
-        greet(device(twin, dx, dy))
+    def on_grid(dx, dy):
+        x, y = gx + dx, gy + dy
+        return (x >= 0) & (x < n_gx) & (y >= 0) & (y < n_gy)
+
+    neighbours = 0
+    for dx, dy in AROUND[::-1]:
+        neighbours = neighbours + jnp.where(on_grid(dx, dy), 1, 0)
+
+        @pl.when(on_grid(dx, dy))
+        def _():
+            greet(device(twin, dx, dy))
+            greet(device(grp, dx, dy))
+
     greet(device(twin, 0, 0))
 
+    held = (fields, stored, material, design, mat_eps, mat_chi, source_wave, source_cells, monitor_cells, owners)
+    given = (
+        fields_in,
+        stored_in,
+        material_in,
+        design_in,
+        mat_eps_in,
+        mat_chi_in,
+        source_wave_in,
+        source_cells_in,
+        monitor_cells_in,
+        owners_in,
+    )
+    loads = [pltpu.make_async_copy(a, b, load_sem.at[i]) for i, (a, b) in enumerate(zip(given, held))]
+    for load in loads:
+        load.start()
+
     @pl.when(forward)
     def _():
-        def column(i, carry):
-            greet({"grp": 2 + i // n_gy, "gx": gx, "gy": lax.rem(i, n_gy)})
-            return carry
-
-        lax.fori_loop(0, 2 * n_gy, column, 0)
+        for j in range(n_gy):
+            for lane in (2, 3):
+                greet({"grp": lane, "gx": gx, "gy": lax.rem(gy + far_first(n_gy)[j], n_gy)})
 
     @pl.when(jnp.logical_not(forward))
     def _():
-        def line(j, carry):
+        for j in far_first(n_gy):
+            for lane in range(4):
+                if j + lane:
+                    greet(device(lax.rem(grp + lane, 4), 0, j))
+        for j in far_first(n_gx)[:-1]:
             greet(device(grp, j, 0))
-            return carry
-
-        lax.fori_loop(1, n_gx, line, 0)
-
-        def column(i, carry):
-            greet(device(lax.rem(grp + i // n_gy, 4), 0, lax.rem(i, n_gy)))
-            return carry
-
-        lax.fori_loop(1, 4 * n_gy, column, 0)
+
+    for i, (dx, dy) in enumerate(AROUND):
+        x, y = gx - dx, gy - dy
+
+        @pl.when((x < 0) | (x >= n_gx) | (y < 0) | (y >= n_gy))
+        def _():
+            if i < 2:
+                row_in[i] = jnp.zeros(row_in.shape[1:], F32)
+                rowh_in[i] = jnp.zeros(rowh_in.shape[1:], BF16)
+                rowc_in[i] = jnp.zeros(rowc_in.shape[1:], BF16)
+                return
+            if i < 4:
+                col_in[i - 2] = jnp.zeros(col_in.shape[1:], F32)
+            else:
+                corner_in[i - 4] = jnp.zeros(corner_in.shape[1:], F32)
+            colh_in[i - 2] = jnp.zeros(colh_in.shape[1:], BF16)
+            colc_in[i - 2] = jnp.zeros(colc_in.shape[1:], BF16)
 
     def lookup(index, entries):
         value = jnp.zeros(index.shape, F32)
@@ -206,15 +278,14 @@
             value = jnp.where(index == k, entries[k], value)
         return value
 
-    kinds = [material[z] for z in range(NZ)]
-    eps = [lookup(kinds[z], mat_eps) + design[...] for z in range(NZ)]
-    chi = [lookup(kinds[z], mat_chi) for z in range(NZ)]
-    own = [fields[c, z] for c in range(6) for z in range(NZ)] + eps + chi
-    col_out[...] = pack_columns(own)
-    for i in range(8):
-        row_out[0, i], row_out[1, i] = pack_rows(own[2 * i], own[2 * i + 1])
-
-    pl.semaphore_wait(barrier, jnp.where(forward, 17 + 2 * n_gy, 17 + n_gx - 1 + 4 * n_gy - 1))
+    def own_planes():
+        kinds = [material[z] for z in range(NZ)]
+        eps = [lookup(kinds[z], mat_eps) + design[...] for z in range(NZ)]
+        chi = [lookup(kinds[z], mat_chi) for z in range(NZ)]
+        return [fields[c, z] for c in range(6) for z in range(NZ)] + eps + chi
+
+    def half_planes(k, components):
+        return [stored[k, c, z].astype(F32) for c in range(components) for z in range(NZ)]
 
     def row_copy(i):
         return pltpu.make_async_remote_copy(
@@ -250,48 +321,106 @@
     def rim_copies():
         return [row_copy(0), row_copy(1), col_copy(2), col_copy(3)] + [corner_copy(i) for i in range(4, 8)]
 
-    for copy in rim_copies():
-        copy.start()
-
-    for k in range(HALF):
-        planes = [stored[k, c, z].astype(F32) for c in range(6) for z in range(NZ)]
-        colh_out[k] = pack_columns(planes).astype(BF16)
-        for i in range(3):
-            one = pack_rows(planes[4 * i], planes[4 * i + 1])
-            two = pack_rows(planes[4 * i + 2], planes[4 * i + 3])
-            for side in range(2):
-                rowh_out[side, 3 * k + i] = jnp.concatenate([one[side], two[side]], axis=0).astype(BF16)
-
-    def half_copy(which, i):
+    def half_copy(k, i):
         if i < 2:
-            src, dst = rowh_out.at[i], rowh_in.at[which, i]
+            src, dst = rowh_out.at[i, k], rowh_in.at[i, k]
         else:
-            src, dst = colh_out, colh_in.at[which, i - 2]
+            src, dst = colh_out.at[k], colh_in.at[i - 2, k]
         return pltpu.make_async_remote_copy(
             src_ref=src,
             dst_ref=dst,
-            send_sem=ownh_sem.at[i],
-            recv_sem=inh_sem.at[which, i],
-            device_id=device(half_lane, *AROUND[i]),
+            send_sem=ownh_sem.at[k, i],
+            recv_sem=inh_sem.at[k, i],
+            device_id=device(grp, *AROUND[i]),
             device_id_type=MESH,
         )
 
-    for i in range(8):
-        half_copy(ahead, i).start()
-
-    def whole_half():
+    def thin_copy(i):
+        if i < 2:
+            src, dst = rowc_out.at[i], rowc_in.at[i]
+        else:
+            src, dst = colc_out, colc_in.at[i - 2]
         return pltpu.make_async_remote_copy(
-            src_ref=stored,
-            dst_ref=half_in,
-            send_sem=half_send,
-            recv_sem=half_sem,
-            device_id=device(half_lane, 0, 0),
+            src_ref=src,
+            dst_ref=dst,
+            send_sem=thin_send.at[i],
+            recv_sem=thin_sem.at[i],
+            device_id=device(twin, *AROUND[i]),
             device_id_type=MESH,
         )
 
+    def whole_half(k):
+        return pltpu.make_async_remote_copy(
+            src_ref=stored.at[k],
+            dst_ref=half_in.at[k],
+            send_sem=half_send.at[k],
+            recv_sem=half_sem.at[k],
+            device_id=device(twin, 0, 0),
+            device_id_type=MESH,
+        )
+
+    def sent(i, act):
+        pl.when(on_grid(*AROUND[i]))(act)
+
+    def received(i, act):
+        dx, dy = AROUND[i]
+        pl.when(on_grid(-dx, -dy))(act)
+
+    def send_rims():
+        for i, copy in enumerate(rim_copies()):
+            sent(i, copy.start)
+
+    def pack_rims():
+        planes = own_planes()
+        col_out[...] = pack_columns(planes)
+        for i in range(8):
+            row_out[0, i], row_out[1, i] = pack_rows(planes[2 * i], planes[2 * i + 1])
+
+    def all_in():
+        pl.semaphore_wait(barrier, 2 * neighbours + 1 + jnp.where(forward, 2 * n_gy, n_gx - 1 + 4 * n_gy - 1))
+
+    stored_load = loads.pop(1)
+
     @pl.when(forward)
     def _():
-        whole_half().start()
+        stored_load.wait()
+        planes = half_planes(1, 6) + half_planes(0, 3)
+        colc_out[...] = pack_columns(planes, RIM).astype(BF16)
+        parts = [pack_thin_rows(planes[i : i + 4]) for i in range(0, len(planes), 4)]
+        parts.append(parts[-1])
+        for i in range(3):
+            for side in range(2):
+                rowc_out[side, i] = jnp.concatenate(
+                    [parts[2 * i][side], parts[2 * i + 1][side]], axis=0
+                ).astype(BF16)
+        all_in()
+        for i in range(8):
+            sent(i, thin_copy(i).start)
+        for k in range(HALF - 1, -1, -1):
+            whole_half(k).start()
+        for load in loads:
+            load.wait()
+        pack_rims()
+        send_rims()
+
+    @pl.when(jnp.logical_not(forward))
+    def _():
+        for load in loads:
+            load.wait()
+        pack_rims()
+        all_in()
+        send_rims()
+        stored_load.wait()
+        for k in range(HALF - 1, -1, -1):
+            planes = half_planes(k, 6)
+            colh_out[k] = pack_columns(planes).astype(BF16)
+            for i in range(3):
+                one = pack_rows(planes[4 * i], planes[4 * i + 1])
+                two = pack_rows(planes[4 * i + 2], planes[4 * i + 3])
+                for side in range(2):
+                    rowh_out[side, k, i] = jnp.concatenate([one[side], two[side]], axis=0).astype(BF16)
+            for i in range(8):
+                sent(i, half_copy(k, i).start)
 
     row = iota((NZ * EX, TY), 0)
     depth = jnp.where(row >= EX, 1, 0)
@@ -361,14 +490,15 @@
     step = jnp.where(inside, DT, 0.0)
     counts = [counts_ref[z * EX : (z + 1) * EX] for z in range(NZ)]
 
-    for copy in rim_copies():
-        copy.wait_recv()
+    for i, copy in enumerate(rim_copies()):
+        received(i, copy.wait_recv)
+    own = own_planes()
     columns = merge_columns(col_in[0], col_in[1], [corner_in[i] for i in range(4)])
     whole = []
     for i in range(8):
         for k, rows in enumerate(unpack_rows(row_in[0, i], row_in[1, i])):
-            whole.append(extended(own[2 * i + k], rows, columns, 2 * i + k))
-    eps = whole[12:14]
+            whole.append(extended(own[2 * i + k], rows, columns, 8 * (2 * i + k)))
+    eps = [jnp.where(inside, v, 1.0) for v in whole[12:14]]
     chi = whole[14:16]
     whole = [jnp.where(inside, v, 0.0) for v in whole[:12]]
     first = [whole[2 * c : 2 * c + 2] for c in range(3)]
@@ -390,7 +520,7 @@
             dst_ref=stored_next.at[n - HALF],
             send_sem=record_send.at[n - HALF],
             recv_sem=record_sem.at[n - HALF],
-            device_id=device(half_lane, 0, 0),
+            device_id=device(twin, 0, 0),
             device_id_type=MESH,
         )
 
@@ -418,57 +548,34 @@
             electric[0] = [electric[0][z] + wave * counts[z] for z in range(NZ)]
         finish(electric, magnetic)
 
-    def rims_of_half(which, k):
+    def corners_of(packed):
+        return [packed[2][:8], packed[3][:8], packed[4][8:], packed[5][8:]]
+
+    def vectors(planes):
+        return [planes[2 * c : 2 * c + 2] for c in range(len(planes) // 2)]
+
+    def late_snapshot(k):
         rows = []
         for i in range(3):
-            after = rowh_in[which, 0, 3 * k + i].astype(F32)
-            before = rowh_in[which, 1, 3 * k + i].astype(F32)
+            after, before = rowh_in[0, k, i].astype(F32), rowh_in[1, k, i].astype(F32)
             rows.extend(unpack_rows(after[:8], before[:8]))
             rows.extend(unpack_rows(after[8:], before[8:]))
-        packed = [colh_in[which, i, k].astype(F32) for i in range(6)]
-        corners = [packed[2][:8], packed[3][:8], packed[4][8:], packed[5][8:]]
-        return rows, merge_columns(packed[0], packed[1], corners)
-
-    def snapshot(which, k):
-        tile = stored if which == 0 else half_in
-        rows, columns = rims_of_half(which, k)
-        planes = [
-            extended(tile[k, c, z].astype(F32), rows[2 * c + z], columns, 2 * c + z)
-            for c in range(6)
-            for z in range(NZ)
-        ]
-        past = [planes[2 * c : 2 * c + 2] for c in range(3)]
-        curled = [planes[2 * c : 2 * c + 2] for c in range(3, 6)]
-        return past, curled
-
-    @pl.when(jnp.logical_not(forward))
-    def _():
-        electric, magnetic = first, second
-        gradient = jnp.zeros((TX, TY), F32)
-        for n in range(STEPS - 1, -1, -1):
-            which, k = (0, n - HALF) if n >= HALF else (1, n)
-            if k == HALF - 1:
-                for i in range(8):
-                    half_copy(which, i).wait_recv()
-                if which == 1:
-                    whole_half().wait_recv()
-            past, curled = snapshot(which, k)
-            factor = [DT / (eps[z] + chi[z] * square(past, z)) for z in range(NZ)]
-            inner = [
-                curled[0][z] * electric[0][z] + curled[1][z] * electric[1][z] + curled[2][z] * electric[2][z]
-                for z in range(NZ)
-            ]
-            turn = curl_up([[factor[z] * electric[c][z] for z in range(NZ)] for c in range(3)])
-            magnetic = [[magnetic[c][z] + unit * turn[c][z] for z in range(NZ)] for c in range(3)]
-            turn = curl_down(magnetic)
-            slope = [factor[z] * factor[z] * inner[z] for z in range(NZ)]
-            gradient = gradient - (1.0 / DT) * (slope[0] + slope[1])[:TX, :TY]
-            weight = [counts[z] - (2.0 / DT) * chi[z] * slope[z] for z in range(NZ)]
-            electric = [
-                [electric[c][z] + weight[z] * past[c][z] - step * turn[c][z] for z in range(NZ)] for c in range(3)
-            ]
-        tiles[0] = gradient
-        finish(electric, magnetic)
+        packed = [colh_in[i, k].astype(F32) for i in range(6)]
+        columns = merge_columns(packed[0], packed[1], corners_of(packed))
+        return vectors([extended(v, rows[p], columns, 8 * p) for p, v in enumerate(half_planes(k, 6))])
+
+    def early_snapshot(k, columns):
+        planes = []
+        for p in range(12):
+            tile = half_in[k, p // NZ, p % NZ].astype(F32)
+            place = p if k else 12 + p
+            if place >= 18:
+                planes.append(extended(tile, jnp.zeros((8, TY), F32), jnp.zeros((EX, TY), F32), 0))
+                continue
+            slot = slice(8 * (place // 4 % 2), 8 * (place // 4 % 2) + 8)
+            after, before = [rowc_in[side, place // 8].astype(F32)[slot] for side in range(2)]
+            planes.append(extended(tile, unpack_thin_rows(after, before, place % 4), columns, RIM * place))
+        return vectors(planes)
 
     def tile_copy(j):
         return pltpu.make_async_remote_copy(
@@ -490,6 +597,44 @@
             device_id_type=MESH,
         )
 
+    @pl.when(jnp.logical_not(forward))
+    def _():
+        electric, magnetic = first, second
+        gradient = jnp.zeros((TX, TY), F32)
+        for n in range(STEPS - 1, -1, -1):
+            if n >= HALF:
+                for i in range(8):
+                    received(i, half_copy(n - HALF, i).wait_recv)
+                snapshot = late_snapshot(n - HALF)
+            else:
+                whole_half(n).wait_recv()
+                if n == HALF - 1:
+                    for i in range(8):
+                        received(i, thin_copy(i).wait_recv)
+                    packed = [colc_in[i].astype(F32) for i in range(6)]
+                    columns = merge_columns(packed[0], packed[1], corners_of(packed), RIM)
+                snapshot = early_snapshot(n, columns)
+            past, curled = snapshot[:3], snapshot[3:]
+            factor = [DT / (eps[z] + chi[z] * square(past, z)) for z in range(NZ)]
+            inner = [
+                curled[0][z] * electric[0][z] + curled[1][z] * electric[1][z] + curled[2][z] * electric[2][z]
+                for z in range(NZ)
+            ]
+            slope = [factor[z] * factor[z] * inner[z] for z in range(NZ)]
+            gradient = gradient - (1.0 / DT) * (slope[0] + slope[1])[:TX, :TY]
+            if n == 0:
+                tiles[0] = gradient
+                for j in far_first(n_gx)[:-1]:
+                    tile_copy(j).start()
+            turn = curl_up([[factor[z] * electric[c][z] for z in range(NZ)] for c in range(3)])
+            magnetic = [[magnetic[c][z] + unit * turn[c][z] for z in range(NZ)] for c in range(3)]
+            turn = curl_down(magnetic)
+            weight = [counts[z] - (2.0 / DT) * chi[z] * slope[z] for z in range(NZ)]
+            electric = [
+                [electric[c][z] + weight[z] * past[c][z] - step * turn[c][z] for z in range(NZ)] for c in range(3)
+            ]
+        finish(electric, magnetic)
+
     def each(low, high, act):
         def body(i, carry):
             act(i)
@@ -499,8 +644,8 @@
 
     @pl.when(jnp.logical_not(forward))
     def _():
-        each(1, n_gx, lambda j: tile_copy(j).start())
-        each(1, n_gx, lambda j: tile_copy(j).wait_recv())
+        for j in range(1, n_gx):
+            tile_copy(j).wait_recv()
         rest = jnp.concatenate([tiles[j] for j in range(n_gx)], axis=0)
         total = jnp.zeros((4 * n_gy * SHARE, TY), F32)
         for _ in range(3):
@@ -510,7 +655,10 @@
         for i in range(4 * n_gy):
             shares[i] = total[SHARE * i : SHARE * (i + 1)]
         gathered[0] = total[:SHARE]
-        each(1, 4 * n_gy, lambda i: share_copy(i).start())
+        for j in far_first(n_gy):
+            for lane in (2, 1, 3, 0):
+                if lane + j:
+                    share_copy(lane * n_gy + j).start()
 
     sum_of = jnp.zeros((SHARE, TY), F32)
     for lane in (2, 3):
@@ -520,15 +668,16 @@
             sum_of = sum_of + gathered[start + j]
     design_grad[...] = sum_of
 
-    for copy in rim_copies():
-        copy.wait_send()
-    for i in range(8):
-        half_copy(ahead, i).wait_send()
+    for i, copy in enumerate(rim_copies()):
+        sent(i, copy.wait_send)
     state_copy().wait()
 
     @pl.when(forward)
     def _():
-        whole_half().wait_send()
+        for k in range(HALF):
+            whole_half(k).wait_send()
+        for i in range(8):
+            sent(i, thin_copy(i).wait_send)
         for n in range(STEPS):
             if n < HALF:
                 kept_copy(n).wait()
@@ -537,39 +686,63 @@
 
     @pl.when(jnp.logical_not(forward))
     def _():
+        for k in range(HALF):
+            for i in range(8):
+                sent(i, half_copy(k, i).wait_send)
         for n in range(HALF, STEPS):
             record_copy(n).wait_recv()
-        each(1, n_gx, lambda j: tile_copy(j).wait_send())
-        each(1, 4 * n_gy, lambda i: share_copy(i).wait_send())
+        for j in range(1, n_gx):
+            tile_copy(j).wait_send()
+        for i in range(1, 4 * n_gy):
+            share_copy(i).wait_send()
+
+
+def store(fields, stored, design_grad, fields_next, stored_next, design_grad_next):
+    fields_next[...] = fields[...]
+    stored_next[...] = stored[...]
+    design_grad_next[...] = design_grad[...]
 
 
 def local(fields, stored, material, design, mat_eps, mat_chi, source_wave, source_cells, monitor_cells, owners):
     n_gx, n_gy = lax.axis_size("gx"), lax.axis_size("gy")
     vmem = pl.BlockSpec(memory_space=pltpu.VMEM)
-    smem = pl.BlockSpec(memory_space=pltpu.SMEM)
-    anywhere = pl.BlockSpec(memory_space=pl.ANY)
+    hbm = pl.BlockSpec(memory_space=pltpu.HBM)
     dma = pltpu.SemaphoreType.DMA
     cells = source_cells.shape[0]
-    fields_next, stored_next, design_grad = pl.pallas_call(
+    outs = pl.pallas_call(
         functools.partial(kernel, n_gx, n_gy),
         out_shape=(
             jax.ShapeDtypeStruct((6, NZ, TX, TY), F32),
             jax.ShapeDtypeStruct((HALF, 6, NZ, TX, TY), BF16),
             jax.ShapeDtypeStruct((SHARE, TY), F32),
         ),
-        in_specs=[vmem, vmem, vmem, vmem, smem, smem, smem, vmem, vmem, vmem],
-        out_specs=(anywhere, anywhere, vmem),
+        in_specs=[hbm] * 10,
+        out_specs=(hbm, hbm, vmem),
         scratch_shapes=[
+            pltpu.VMEM((6, NZ, TX, TY), F32),
+            pltpu.VMEM((HALF, 6, NZ, TX, TY), BF16),
+            pltpu.VMEM((NZ, TX, TY), jnp.int32),
+            pltpu.VMEM((TX, TY), F32),
+            pltpu.SMEM((4,), F32),
+            pltpu.SMEM((4,), F32),
+            pltpu.SMEM((2, STEPS), F32),
+            pltpu.VMEM((cells // TY, TY), jnp.int32),
+            pltpu.VMEM((cells // TY, TY), jnp.int32),
+            pltpu.VMEM((n_gx, TX * n_gy), jnp.int32),
             pltpu.VMEM((TX, TY), F32),
             pltpu.VMEM((HALF, TX, TY), BF16),
             pltpu.VMEM((2, 8, 8, TY), F32),
-            pltpu.VMEM((2, 6, TX, TY), BF16),
+            pltpu.VMEM((2, HALF, 3, TX, TY), BF16),
             pltpu.VMEM((2, TX, TY), F32),
             pltpu.VMEM((4, 8, TY), F32),
             pltpu.VMEM((2, 8, 8, TY), F32),
-            pltpu.VMEM((2, 6, HALF, TX, TY), BF16),
-            pltpu.VMEM((2, 2, 6, TX, TY), BF16),
+            pltpu.VMEM((6, HALF, TX, TY), BF16),
+            pltpu.VMEM((2, HALF, 3, TX, TY), BF16),
             pltpu.VMEM((HALF, 6, NZ, TX, TY), BF16),
+            pltpu.VMEM((2, 3, TX, TY), BF16),
+            pltpu.VMEM((2, 3, TX, TY), BF16),
+            pltpu.VMEM((TX, TY), BF16),
+            pltpu.VMEM((6, TX, TY), BF16),
             pltpu.VMEM((STEPS, 6, NZ, TX, TY), BF16),
             pltpu.VMEM((6, NZ, TX, TY), F32),
             pltpu.VMEM((NZ * EX, EY), F32),
@@ -578,11 +751,13 @@
             pltpu.VMEM((4 * n_gy, SHARE, TY), F32),
             pltpu.VMEM((4 * n_gy, SHARE, TY), F32),
             dma((8,)),
+            dma((HALF, 8)),
+            dma((HALF,)),
             dma((8,)),
-            dma,
+            dma((HALF, 8)),
+            dma((HALF,)),
             dma((8,)),
-            dma((2, 8)),
-            dma,
+            dma((8,)),
             dma((HALF,)),
             dma((HALF,)),
             dma((n_gx,)),
@@ -590,9 +765,10 @@
             dma((4 * n_gy,)),
             dma((4 * n_gy,)),
             dma((3,)),
+            dma((10,)),
         ],
         compiler_params=pltpu.CompilerParams(
-            collective_id=0, has_side_effects=True, vmem_limit_bytes=32 * 1024 * 1024
+            collective_id=0, has_side_effects=True, vmem_limit_bytes=56 * 1024 * 1024
         ),
         name="interval",
     )(
@@ -607,6 +783,14 @@
         monitor_cells.reshape(cells // TY, TY),
         owners.reshape(n_gx, TX * n_gy),
     )
+    fields_next, stored_next, design_grad = pl.pallas_call(
+        store,
+        out_shape=tuple(jax.ShapeDtypeStruct(a.shape, a.dtype) for a in outs),
+        in_specs=[vmem] * 3,
+        out_specs=(vmem,) * 3,
+        compiler_params=pltpu.CompilerParams(vmem_limit_bytes=56 * 1024 * 1024),
+        name="store",
+    )(*outs)
     return fields_next[None], stored_next[None], design_grad
 
 

time: 57.3 us -> 44.7 us (0.78)
  local copies, waits for them, and re-layouts: 8.44 us -> 0 us
  Pallas kernels: 47.7 us -> 43.9 us
    unnamed x23 -> x0, local copies, waits for them, and re-layouts: 8.44 us -> none
    pallas_call x1, Pallas kernels: 47.7 us -> 42.3 us  [local(): pl.pallas_call(functools.partial(kernel, n_gx, n_gy), out_shape=(jax.Shap...]
    pallas_call x0 -> x1, Pallas kernels: none -> 1.62 us  [local(): pl.pallas_call(store, out_shape=tuple((jax.ShapeDtypeStruct(a.shape, a.dt...]
where the time goes in v2:
time: 44.7 us; the launch traced here: 44.5 us
  Pallas kernels  43.9 us (98%)
  between operations  0.64 us (1%)
    pallas_call x1, Pallas kernels, local(): pl.pallas_call(functools.partial(kernel, n_gx, n_gy), out_shape=(jax.Shap...  42.3 us
    pallas_call x1, Pallas kernels, local(): pl.pallas_call(store, out_shape=tuple((jax.ShapeDtypeStruct(a.shape, a.dt...  1.62 us

profile of v2, /device:TPU:1, one launch (start us, length us, event | category | flops | bytes accessed | tf_op | source)
XLA Modules:
  0.0 44.5 jit_solution(8032955026075770689)
XLA Ops:
  0.6 42.3 %interval.1 = (f32[6,2,16,128]{3,2,1,0:T(8,128)}, bf16[2,6,2,16,128]{4,3,2,1,0:T(8,128)(2,1)}, f32[4,128]{1,0:T(4,128)}) custom-call(f32[6,2,16,128]{3,2,1,0:T(8,128)} %bitcast.7, bf16[2,6,2,16,128]{4,3,2,1,0:T(8,128)(2,1)} %bitcast.8, s32[2,16,128]{2,1,0:T(8,128)} %material_in.1, f32[16,128]{1,0:T(8,128)} %design_in.1, f32[4]{0:T(128)} %mat_eps_in.1, ...), custom_call_target="tpu_custom_call" | custom-call | tf_op jit(solution)/shard_map/interval/pallas_call | solution.py:712
  42.9 1.6 %store.1 = (f32[6,2,16,128]{3,2,1,0:T(8,128)}, bf16[2,6,2,16,128]{4,3,2,1,0:T(8,128)(2,1)}, f32[4,128]{1,0:T(4,128)}) custom-call(f32[6,2,16,128]{3,2,1,0:T(8,128)} %get-tuple-element.9.fields, bf16[2,6,2,16,128]{4,3,2,1,0:T(8,128)(2,1)} %get-tuple-element.10.stored, f32[4,128]{1,0:T(4,128)} %get-tuple-element.11.design_grad), custom_call_target="tpu_custom_call" | custom-call | tf_op jit(solution)/shard_map/store/pallas_call | solution.py:786

commit v3 on v2

--- a/solution.py
+++ b/solution.py
@@ -1,4 +1,5 @@
 import functools
+import math
 
 import jax
 import jax.numpy as jnp
@@ -143,7 +144,7 @@
     owners_in,
     fields_next,
     stored_next,
-    design_grad,
+    gathered,
     fields,
     stored,
     material,
@@ -168,13 +169,14 @@
     rowc_in,
     colc_out,
     colc_in,
+    rowc_here,
+    colc_here,
     records,
     state,
     counts_ref,
     chosen,
     tiles,
     shares,
-    gathered,
     own_sem,
     ownh_sem,
     half_send,
@@ -183,6 +185,10 @@
     half_sem,
     thin_send,
     thin_sem,
+    hand_send,
+    hand_sem,
+    second_round,
+    third_round,
     record_send,
     record_sem,
     tile_send,
@@ -204,24 +210,47 @@
         }
 
     barrier = pltpu.get_barrier_semaphore()
-
-    def greet(target):
-        pl.semaphore_signal(barrier, inc=1, device_id=target, device_id_type=MESH)
+    side = math.isqrt(n_gx)
 
     def on_grid(dx, dy):
         x, y = gx + dx, gy + dy
         return (x >= 0) & (x < n_gx) & (y >= 0) & (y < n_gy)
 
+    def greet(target):
+        pl.semaphore_signal(barrier, inc=1, device_id=target, device_id_type=MESH)
+
+    def in_row(d):
+        return {"grp": grp, "gx": gx - gx % side + (gx + d) % side, "gy": gy}
+
+    def in_pair(d, other):
+        return {"grp": grp, "gx": gx, "gy": lax.rem(gy - gy % 2 + (gy + other) % 2 + 2 * d + n_gy, n_gy)}
+
+    def in_lane(d):
+        return device(lax.rem(grp + d, 4), 0, 0)
+
     neighbours = 0
     for dx, dy in AROUND[::-1]:
-        neighbours = neighbours + jnp.where(on_grid(dx, dy), 1, 0)
-
-        @pl.when(on_grid(dx, dy))
-        def _():
-            greet(device(twin, dx, dy))
-            greet(device(grp, dx, dy))
-
-    greet(device(twin, 0, 0))
+        if dx:
+            neighbours = neighbours + jnp.where(on_grid(dx, dy), 1, 0)
+            pl.when(on_grid(dx, dy))(functools.partial(greet, device(grp, dx, dy)))
+    near = [in_pair(d, other) for d in (-1, 1) for other in (0, 1)] + [in_pair(0, 1)]
+    near += [in_lane(d) for d in range(1, 4)]
+    near += [in_row(d) for d in range(1, side)] + [device(grp, side * d, 0) for d in range(1, n_gx // side)]
+    for target in near:
+        greet(target)
+
+    def all_in():
+        pl.semaphore_wait(barrier, neighbours + len(near))
+        for target in second:
+            pl.semaphore_signal(second_round, inc=1, device_id=target, device_id_type=MESH)
+
+    second = [in_pair(d, 0) for d in (-1, 1)] + [in_row(d) for d in range(1, side)]
+    third = [in_lane(d) for d in range(1, 4)]
+
+    def lane_in():
+        pl.semaphore_wait(second_round, len(second))
+        for target in third:
+            pl.semaphore_signal(third_round, inc=1, device_id=target, device_id_type=MESH)
 
     held = (fields, stored, material, design, mat_eps, mat_chi, source_wave, source_cells, monitor_cells, owners)
     given = (
@@ -240,21 +269,6 @@
     for load in loads:
         load.start()
 
-    @pl.when(forward)
-    def _():
-        for j in range(n_gy):
-            for lane in (2, 3):
-                greet({"grp": lane, "gx": gx, "gy": lax.rem(gy + far_first(n_gy)[j], n_gy)})
-
-    @pl.when(jnp.logical_not(forward))
-    def _():
-        for j in far_first(n_gy):
-            for lane in range(4):
-                if j + lane:
-                    greet(device(lax.rem(grp + lane, 4), 0, j))
-        for j in far_first(n_gx)[:-1]:
-            greet(device(grp, j, 0))
-
     for i, (dx, dy) in enumerate(AROUND):
         x, y = gx - dx, gy - dy
 
@@ -335,17 +349,31 @@
             device_id_type=MESH,
         )
 
+    def thin_copies():
+        pairs = ((rowc_out, rowc_here), (colc_out, colc_here))
+        return [
+            pltpu.make_async_remote_copy(
+                src_ref=src,
+                dst_ref=dst,
+                send_sem=hand_send.at[i],
+                recv_sem=hand_sem.at[i],
+                device_id=device(twin, 0, 0),
+                device_id_type=MESH,
+            )
+            for i, (src, dst) in enumerate(pairs)
+        ]
+
     def thin_copy(i):
         if i < 2:
-            src, dst = rowc_out.at[i], rowc_in.at[i]
+            src, dst = rowc_here.at[i], rowc_in.at[i]
         else:
-            src, dst = colc_out, colc_in.at[i - 2]
+            src, dst = colc_here, colc_in.at[i - 2]
         return pltpu.make_async_remote_copy(
             src_ref=src,
             dst_ref=dst,
             send_sem=thin_send.at[i],
             recv_sem=thin_sem.at[i],
-            device_id=device(twin, *AROUND[i]),
+            device_id=device(grp, *AROUND[i]),
             device_id_type=MESH,
         )
 
@@ -375,9 +403,6 @@
         col_out[...] = pack_columns(planes)
         for i in range(8):
             row_out[0, i], row_out[1, i] = pack_rows(planes[2 * i], planes[2 * i + 1])
-
-    def all_in():
-        pl.semaphore_wait(barrier, 2 * neighbours + 1 + jnp.where(forward, 2 * n_gy, n_gx - 1 + 4 * n_gy - 1))
 
     stored_load = loads.pop(1)
 
@@ -394,13 +419,15 @@
                     [parts[2 * i][side], parts[2 * i + 1][side]], axis=0
                 ).astype(BF16)
         all_in()
-        for i in range(8):
-            sent(i, thin_copy(i).start)
-        for k in range(HALF - 1, -1, -1):
-            whole_half(k).start()
+        for copy in thin_copies():
+            copy.start()
+        whole_half(1).start()
         for load in loads:
             load.wait()
         pack_rims()
+        whole_half(1).wait_send()
+        whole_half(0).start()
+        whole_half(0).wait_send()
         send_rims()
 
     @pl.when(jnp.logical_not(forward))
@@ -490,6 +517,14 @@
     step = jnp.where(inside, DT, 0.0)
     counts = [counts_ref[z * EX : (z + 1) * EX] for z in range(NZ)]
 
+    @pl.when(jnp.logical_not(forward))
+    def _():
+        for copy in thin_copies():
+            copy.wait_recv()
+        for i in range(8):
+            sent(i, thin_copy(i).start)
+
+    lane_in()
     for i, copy in enumerate(rim_copies()):
         received(i, copy.wait_recv)
     own = own_planes()
@@ -586,6 +621,9 @@
             device_id=device(grp, j, 0),
             device_id_type=MESH,
         )
+
+    def own_share():
+        return pltpu.make_async_copy(shares.at[0], gathered.at[0], local_sem.at[3])
 
     def share_copy(i):
         return pltpu.make_async_remote_copy(
@@ -654,19 +692,20 @@
             rest = rest - part.astype(F32)
         for i in range(4 * n_gy):
             shares[i] = total[SHARE * i : SHARE * (i + 1)]
-        gathered[0] = total[:SHARE]
+        own_share().start()
+        pl.semaphore_wait(third_round, len(third))
         for j in far_first(n_gy):
             for lane in (2, 1, 3, 0):
                 if lane + j:
                     share_copy(lane * n_gy + j).start()
 
-    sum_of = jnp.zeros((SHARE, TY), F32)
+    @pl.when(forward)
+    def _():
+        pl.semaphore_wait(third_round, len(third))
+
     for lane in (2, 3):
         start = lax.rem(grp + 4 - lane, 4) * n_gy
         each(start + jnp.where(start == 0, 1, 0), start + n_gy, lambda i: share_copy(i).wait_recv())
-        for j in range(n_gy):
-            sum_of = sum_of + gathered[start + j]
-    design_grad[...] = sum_of
 
     for i, copy in enumerate(rim_copies()):
         sent(i, copy.wait_send)
@@ -674,10 +713,8 @@
 
     @pl.when(forward)
     def _():
-        for k in range(HALF):
-            whole_half(k).wait_send()
-        for i in range(8):
-            sent(i, thin_copy(i).wait_send)
+        for copy in thin_copies():
+            copy.wait_send()
         for n in range(STEPS):
             if n < HALF:
                 kept_copy(n).wait()
@@ -689,18 +726,26 @@
         for k in range(HALF):
             for i in range(8):
                 sent(i, half_copy(k, i).wait_send)
+        for i in range(8):
+            sent(i, thin_copy(i).wait_send)
         for n in range(HALF, STEPS):
             record_copy(n).wait_recv()
         for j in range(1, n_gx):
             tile_copy(j).wait_send()
         for i in range(1, 4 * n_gy):
             share_copy(i).wait_send()
-
-
-def store(fields, stored, design_grad, fields_next, stored_next, design_grad_next):
+        own_share().wait()
+
+
+def store(n_gy, fields, stored, gathered, fields_next, stored_next, design_grad):
     fields_next[...] = fields[...]
     stored_next[...] = stored[...]
-    design_grad_next[...] = design_grad[...]
+    total = jnp.zeros((SHARE, TY), F32)
+    for lane in (2, 3):
+        start = lax.rem(lax.axis_index("grp") + 4 - lane, 4) * n_gy
+        for j in range(n_gy):
+            total = total + gathered[start + j]
+    design_grad[...] = total
 
 
 def local(fields, stored, material, design, mat_eps, mat_chi, source_wave, source_cells, monitor_cells, owners):
@@ -714,10 +759,10 @@
         out_shape=(
             jax.ShapeDtypeStruct((6, NZ, TX, TY), F32),
             jax.ShapeDtypeStruct((HALF, 6, NZ, TX, TY), BF16),
-            jax.ShapeDtypeStruct((SHARE, TY), F32),
+            jax.ShapeDtypeStruct((4 * n_gy, SHARE, TY), F32),
         ),
         in_specs=[hbm] * 10,
-        out_specs=(hbm, hbm, vmem),
+        out_specs=(hbm, hbm, hbm),
         scratch_shapes=[
             pltpu.VMEM((6, NZ, TX, TY), F32),
             pltpu.VMEM((HALF, 6, NZ, TX, TY), BF16),
@@ -743,12 +788,13 @@
             pltpu.VMEM((2, 3, TX, TY), BF16),
             pltpu.VMEM((TX, TY), BF16),
             pltpu.VMEM((6, TX, TY), BF16),
+            pltpu.VMEM((2, 3, TX, TY), BF16),
+            pltpu.VMEM((TX, TY), BF16),
             pltpu.VMEM((STEPS, 6, NZ, TX, TY), BF16),
             pltpu.VMEM((6, NZ, TX, TY), F32),
             pltpu.VMEM((NZ * EX, EY), F32),
             pltpu.VMEM((4 * n_gy * SHARE, n_gx * TX), BF16),
             pltpu.VMEM((n_gx, TX, TY), F32),
-            pltpu.VMEM((4 * n_gy, SHARE, TY), F32),
             pltpu.VMEM((4 * n_gy, SHARE, TY), F32),
             dma((8,)),
             dma((HALF, 8)),
@@ -758,13 +804,17 @@
             dma((HALF,)),
             dma((8,)),
             dma((8,)),
+            dma((2,)),
+            dma((2,)),
+            pltpu.SemaphoreType.REGULAR,
+            pltpu.SemaphoreType.REGULAR,
             dma((HALF,)),
             dma((HALF,)),
             dma((n_gx,)),
             dma((n_gx,)),
             dma((4 * n_gy,)),
             dma((4 * n_gy,)),
-            dma((3,)),
+            dma((4,)),
             dma((10,)),
         ],
         compiler_params=pltpu.CompilerParams(
@@ -784,8 +834,12 @@
         owners.reshape(n_gx, TX * n_gy),
     )
     fields_next, stored_next, design_grad = pl.pallas_call(
-        store,
-        out_shape=tuple(jax.ShapeDtypeStruct(a.shape, a.dtype) for a in outs),
+        functools.partial(store, n_gy),
+        out_shape=(
+            jax.ShapeDtypeStruct(outs[0].shape, F32),
+            jax.ShapeDtypeStruct(outs[1].shape, BF16),
+            jax.ShapeDtypeStruct((SHARE, TY), F32),
+        ),
         in_specs=[vmem] * 3,
         out_specs=(vmem,) * 3,
         compiler_params=pltpu.CompilerParams(vmem_limit_bytes=56 * 1024 * 1024),

time: 44.7 us -> 43.9 us (0.982)
  Pallas kernels: 43.9 us -> 43 us
    pallas_call x1, Pallas kernels: 42.3 us -> 41.4 us  [local(): pl.pallas_call(functools.partial(kernel, n_gx, n_gy), out_shape=(jax.Shap...]
where the time goes in v3:
time: 43.9 us; the launch traced here: 43.7 us
  Pallas kernels  43 us (98%)
  between operations  0.64 us (1%)
    pallas_call x1, Pallas kernels, local(): pl.pallas_call(functools.partial(kernel, n_gx, n_gy), out_shape=(jax.Shap...  41.4 us
    pallas_call x1, Pallas kernels, local(): pl.pallas_call(functools.partial(store, n_gy), out_shape=(jax.ShapeDtypeS...  1.63 us

profile of v3, /device:TPU:1, one launch (start us, length us, event | category | flops | bytes accessed | tf_op | source)
XLA Modules:
  0.0 43.7 jit_solution(3953622519837887636)
XLA Ops:
  0.6 41.4 %interval.1 = (f32[6,2,16,128]{3,2,1,0:T(8,128)}, bf16[2,6,2,16,128]{4,3,2,1,0:T(8,128)(2,1)}, f32[32,4,128]{2,1,0:T(4,128)}) custom-call(f32[6,2,16,128]{3,2,1,0:T(8,128)} %bitcast.7, bf16[2,6,2,16,128]{4,3,2,1,0:T(8,128)(2,1)} %bitcast.8, s32[2,16,128]{2,1,0:T(8,128)} %material_in.1, f32[16,128]{1,0:T(8,128)} %design_in.1, f32[4]{0:T(128)} %mat_eps_in.1, ...), custom_call_target="tpu_custom_call" | custom-call | tf_op jit(solution)/shard_map/interval/pallas_call | solution.py:757
  42.1 1.6 %store.1 = (f32[6,2,16,128]{3,2,1,0:T(8,128)}, bf16[2,6,2,16,128]{4,3,2,1,0:T(8,128)(2,1)}, f32[4,128]{1,0:T(4,128)}) custom-call(f32[6,2,16,128]{3,2,1,0:T(8,128)} %get-tuple-element.9.fields, bf16[2,6,2,16,128]{4,3,2,1,0:T(8,128)(2,1)} %get-tuple-element.10.stored, f32[32,4,128]{2,1,0:T(4,128)} %get-tuple-element.11.gathered), custom_call_target="tpu_custom_call" | custom-call | tf_op jit(solution)/shard_map/store/pallas_call | solution.py:836

commit v4 on v3

--- a/solution.py
+++ b/solution.py
@@ -189,6 +189,8 @@
     hand_sem,
     second_round,
     third_round,
+    fourth_round,
+    go,
     record_send,
     record_sem,
     tile_send,
@@ -210,14 +212,15 @@
         }
 
     barrier = pltpu.get_barrier_semaphore()
+    adjoint = jnp.logical_not(forward)
     side = math.isqrt(n_gx)
 
     def on_grid(dx, dy):
         x, y = gx + dx, gy + dy
         return (x >= 0) & (x < n_gx) & (y >= 0) & (y < n_gy)
 
-    def greet(target):
-        pl.semaphore_signal(barrier, inc=1, device_id=target, device_id_type=MESH)
+    def signal(semaphore, target):
+        pl.semaphore_signal(semaphore, inc=1, device_id=target, device_id_type=MESH)
 
     def in_row(d):
         return {"grp": grp, "gx": gx - gx % side + (gx + d) % side, "gy": gy}
@@ -225,32 +228,41 @@
     def in_pair(d, other):
         return {"grp": grp, "gx": gx, "gy": lax.rem(gy - gy % 2 + (gy + other) % 2 + 2 * d + n_gy, n_gy)}
 
-    def in_lane(d):
-        return device(lax.rem(grp + d, 4), 0, 0)
-
-    neighbours = 0
-    for dx, dy in AROUND[::-1]:
-        if dx:
-            neighbours = neighbours + jnp.where(on_grid(dx, dy), 1, 0)
-            pl.when(on_grid(dx, dy))(functools.partial(greet, device(grp, dx, dy)))
-    near = [in_pair(d, other) for d in (-1, 1) for other in (0, 1)] + [in_pair(0, 1)]
-    near += [in_lane(d) for d in range(1, 4)]
-    near += [in_row(d) for d in range(1, side)] + [device(grp, side * d, 0) for d in range(1, n_gx // side)]
-    for target in near:
-        greet(target)
+    beside = [(dx, dy) for dx, dy in AROUND[::-1] if dx]
+    neighbours = sum(jnp.where(on_grid(dx, dy), 1, 0) for dx, dy in beside)
+    pairs = [in_pair(d, other) for d in (-1, 1) for other in (0, 1)] + [in_pair(0, 1)]
+    rows = [in_row(d) for d in range(1, side)]
+    lines = [device(grp, side * d, 0) for d in range(1, n_gx // side)]
+    other_lane = device(5 - grp, 0, 0)
+
+    def signal_all(semaphore, targets):
+        for dx, dy in beside:
+            pl.when(on_grid(dx, dy))(functools.partial(signal, semaphore, device(grp, dx, dy)))
+        for target in targets:
+            signal(semaphore, target)
+
+    signal(barrier, device(twin, 0, 0))
+
+    @pl.when(adjoint)
+    def _():
+        signal_all(barrier, pairs + rows + lines + [other_lane])
 
     def all_in():
-        pl.semaphore_wait(barrier, neighbours + len(near))
-        for target in second:
-            pl.semaphore_signal(second_round, inc=1, device_id=target, device_id_type=MESH)
-
-    second = [in_pair(d, 0) for d in (-1, 1)] + [in_row(d) for d in range(1, side)]
-    third = [in_lane(d) for d in range(1, 4)]
-
-    def lane_in():
-        pl.semaphore_wait(second_round, len(second))
-        for target in third:
-            pl.semaphore_signal(third_round, inc=1, device_id=target, device_id_type=MESH)
+        first_round = neighbours + len(pairs) + len(rows) + len(lines) + 2
+        pl.semaphore_wait(barrier, jnp.where(forward, 1, first_round))
+
+    def begin_second():
+        signal_all(second_round, pairs + rows)
+
+    def end_second():
+        pl.semaphore_wait(second_round, neighbours + len(pairs) + len(rows))
+        signal(go, device(twin, 0, 0))
+        for d in (-1, 1):
+            signal(third_round, in_pair(d, 0))
+
+    def end_third():
+        pl.semaphore_wait(third_round, 2)
+        signal(fourth_round, other_lane)
 
     held = (fields, stored, material, design, mat_eps, mat_chi, source_wave, source_cells, monitor_cells, owners)
     given = (
@@ -427,16 +439,15 @@
         pack_rims()
         whole_half(1).wait_send()
         whole_half(0).start()
-        whole_half(0).wait_send()
-        send_rims()
-
-    @pl.when(jnp.logical_not(forward))
+
+    @pl.when(adjoint)
     def _():
         for load in loads:
             load.wait()
         pack_rims()
         all_in()
         send_rims()
+        begin_second()
         stored_load.wait()
         for k in range(HALF - 1, -1, -1):
             planes = half_planes(k, 6)
@@ -486,7 +497,7 @@
 
     counts_ref[...] = jnp.concatenate([tally(rows_hit, columns_hit), tally(rows_hit, rim_hit)], axis=1)
 
-    @pl.when(jnp.logical_not(forward))
+    @pl.when(adjoint)
     def _():
         lanes = owners.shape[1]
         pick = iota((TX, lanes), 1) == iota((TX, lanes), 0) * n_gy + gy
@@ -517,14 +528,19 @@
     step = jnp.where(inside, DT, 0.0)
     counts = [counts_ref[z * EX : (z + 1) * EX] for z in range(NZ)]
 
-    @pl.when(jnp.logical_not(forward))
+    @pl.when(adjoint)
     def _():
         for copy in thin_copies():
             copy.wait_recv()
         for i in range(8):
             sent(i, thin_copy(i).start)
-
-    lane_in()
+        end_second()
+
+    @pl.when(forward)
+    def _():
+        pl.semaphore_wait(go, 1)
+        send_rims()
+
     for i, copy in enumerate(rim_copies()):
         received(i, copy.wait_recv)
     own = own_planes()
@@ -635,7 +651,7 @@
             device_id_type=MESH,
         )
 
-    @pl.when(jnp.logical_not(forward))
+    @pl.when(adjoint)
     def _():
         electric, magnetic = first, second
         gradient = jnp.zeros((TX, TY), F32)
@@ -680,8 +696,9 @@
 
         lax.fori_loop(low, high, body, 0)
 
-    @pl.when(jnp.logical_not(forward))
-    def _():
+    @pl.when(adjoint)
+    def _():
+        end_third()
         for j in range(1, n_gx):
             tile_copy(j).wait_recv()
         rest = jnp.concatenate([tiles[j] for j in range(n_gx)], axis=0)
@@ -693,16 +710,12 @@
         for i in range(4 * n_gy):
             shares[i] = total[SHARE * i : SHARE * (i + 1)]
         own_share().start()
-        pl.semaphore_wait(third_round, len(third))
+        pl.semaphore_wait(fourth_round, 1)
         for j in far_first(n_gy):
             for lane in (2, 1, 3, 0):
                 if lane + j:
                     share_copy(lane * n_gy + j).start()
 
-    @pl.when(forward)
-    def _():
-        pl.semaphore_wait(third_round, len(third))
-
     for lane in (2, 3):
         start = lax.rem(grp + 4 - lane, 4) * n_gy
         each(start + jnp.where(start == 0, 1, 0), start + n_gy, lambda i: share_copy(i).wait_recv())
@@ -715,13 +728,15 @@
     def _():
         for copy in thin_copies():
             copy.wait_send()
+        for k in range(HALF - 1):
+            whole_half(k).wait_send()
         for n in range(STEPS):
             if n < HALF:
                 kept_copy(n).wait()
             else:
                 record_copy(n).wait_send()
 
-    @pl.when(jnp.logical_not(forward))
+    @pl.when(adjoint)
     def _():
         for k in range(HALF):
             for i in range(8):
@@ -808,6 +823,8 @@
             dma((2,)),
             pltpu.SemaphoreType.REGULAR,
             pltpu.SemaphoreType.REGULAR,
+            pltpu.SemaphoreType.REGULAR,
+            pltpu.SemaphoreType.REGULAR,
             dma((HALF,)),
             dma((HALF,)),
             dma((n_gx,)),

time: 43.9 us -> 39.7 us (0.904)
  Pallas kernels: 43 us -> 38.9 us
    pallas_call x1, Pallas kernels: 41.4 us -> 37.2 us  [local(): pl.pallas_call(functools.partial(kernel, n_gx, n_gy), out_shape=(jax.Shap...]
where the time goes in v4:
time: 39.7 us; the launch traced here: 39.5 us
  Pallas kernels  38.9 us (98%)
  between operations  0.64 us (2%)
    pallas_call x1, Pallas kernels, local(): pl.pallas_call(functools.partial(kernel, n_gx, n_gy), out_shape=(jax.Shap...  37.2 us
    pallas_call x1, Pallas kernels, local(): pl.pallas_call(functools.partial(store, n_gy), out_shape=(jax.ShapeDtypeS...  1.63 us

profile of v4, /device:TPU:1, one launch (start us, length us, event | category | flops | bytes accessed | tf_op | source)
XLA Modules:
  0.0 39.5 jit_solution(308574065779100277)
XLA Ops:
  0.6 37.2 %interval.1 = (f32[6,2,16,128]{3,2,1,0:T(8,128)}, bf16[2,6,2,16,128]{4,3,2,1,0:T(8,128)(2,1)}, f32[32,4,128]{2,1,0:T(4,128)}) custom-call(f32[6,2,16,128]{3,2,1,0:T(8,128)} %bitcast.7, bf16[2,6,2,16,128]{4,3,2,1,0:T(8,128)(2,1)} %bitcast.8, s32[2,16,128]{2,1,0:T(8,128)} %material_in.1, f32[16,128]{1,0:T(8,128)} %design_in.1, f32[4]{0:T(128)} %mat_eps_in.1, ...), custom_call_target="tpu_custom_call" | custom-call | tf_op jit(solution)/shard_map/interval/pallas_call | solution.py:772
  37.9 1.6 %store.1 = (f32[6,2,16,128]{3,2,1,0:T(8,128)}, bf16[2,6,2,16,128]{4,3,2,1,0:T(8,128)(2,1)}, f32[4,128]{1,0:T(4,128)}) custom-call(f32[6,2,16,128]{3,2,1,0:T(8,128)} %get-tuple-element.9.fields, bf16[2,6,2,16,128]{4,3,2,1,0:T(8,128)(2,1)} %get-tuple-element.10.stored, f32[32,4,128]{2,1,0:T(4,128)} %get-tuple-element.11.gathered), custom_call_target="tpu_custom_call" | custom-call | tf_op jit(solution)/shard_map/store/pallas_call | solution.py:853

commit v5 on v4

--- a/solution.py
+++ b/solution.py
@@ -172,7 +172,6 @@
     rowc_here,
     colc_here,
     records,
-    state,
     counts_ref,
     chosen,
     tiles,
@@ -197,7 +196,6 @@
     tile_sem,
     share_send,
     share_sem,
-    local_sem,
     load_sem,
 ):
     grp, gx, gy = lax.axis_index("grp"), lax.axis_index("gx"), lax.axis_index("gy")
@@ -224,6 +222,14 @@
 
     def in_row(d):
         return {"grp": grp, "gx": gx - gx % side + (gx + d) % side, "gy": gy}
+
+    def line_far_first():
+        def across(place, c):
+            return (place, place + 1 - 2 * (place % 2), (place + 2) % 4, 3 - place)[c]
+
+        codes = [(a, b) for a in range(n_gx // side) for b in range(side)]
+        for a, b in sorted(codes, key=lambda code: -sum(code))[:-1]:
+            yield lax.rem(across(gx // side, a) * side + across(gx % side, b) - gx + n_gx, n_gx)
 
     def in_pair(d, other):
         return {"grp": grp, "gx": gx, "gy": lax.rem(gy - gy % 2 + (gy + other) % 2 + 2 * d + n_gy, n_gy)}
@@ -407,7 +413,7 @@
         pl.when(on_grid(-dx, -dy))(act)
 
     def send_rims():
-        for i, copy in enumerate(rim_copies()):
+        for i, copy in list(enumerate(rim_copies()))[::-1]:
             sent(i, copy.start)
 
     def pack_rims():
@@ -457,7 +463,7 @@
                 two = pack_rows(planes[4 * i + 2], planes[4 * i + 3])
                 for side in range(2):
                     rowh_out[side, k, i] = jnp.concatenate([one[side], two[side]], axis=0).astype(BF16)
-            for i in range(8):
+            for i in range(7, -1, -1):
                 sent(i, half_copy(k, i).start)
 
     row = iota((NZ * EX, TY), 0)
@@ -532,7 +538,7 @@
     def _():
         for copy in thin_copies():
             copy.wait_recv()
-        for i in range(8):
+        for i in range(7, -1, -1):
             sent(i, thin_copy(i).start)
         end_second()
 
@@ -555,28 +561,21 @@
     first = [whole[2 * c : 2 * c + 2] for c in range(3)]
     second = [whole[2 * c : 2 * c + 2] for c in range(3, 6)]
 
-    def state_copy():
-        return pltpu.make_async_copy(state, fields_next, local_sem.at[0])
-
     def finish(electric, magnetic):
         for c in range(3):
             for z in range(NZ):
-                state[c, z] = electric[c][z][:TX, :TY]
-                state[3 + c, z] = magnetic[c][z][:TX, :TY]
-        state_copy().start()
+                fields_next[c, z] = electric[c][z][:TX, :TY]
+                fields_next[3 + c, z] = magnetic[c][z][:TX, :TY]
 
     def record_copy(n):
         return pltpu.make_async_remote_copy(
-            src_ref=records.at[n],
+            src_ref=records.at[n - HALF],
             dst_ref=stored_next.at[n - HALF],
             send_sem=record_send.at[n - HALF],
             recv_sem=record_sem.at[n - HALF],
             device_id=device(twin, 0, 0),
             device_id_type=MESH,
         )
-
-    def kept_copy(n):
-        return pltpu.make_async_copy(records.at[n], stored_next.at[n], local_sem.at[1 + n])
 
     def square(v, z):
         return v[0][z] * v[0][z] + v[1][z] * v[1][z] + v[2][z] * v[2][z]
@@ -591,9 +590,11 @@
             turn = curl_down(magnetic)
             for c in range(3):
                 for z in range(NZ):
-                    records[n, c, z] = electric[c][z][:TX, :TY].astype(BF16)
-                    records[n, 3 + c, z] = turn[c][z][:TX, :TY].astype(BF16)
-            (kept_copy if n < HALF else record_copy)(n).start()
+                    record = stored_next if n < HALF else records
+                    record[n % HALF, c, z] = electric[c][z][:TX, :TY].astype(BF16)
+                    record[n % HALF, 3 + c, z] = turn[c][z][:TX, :TY].astype(BF16)
+            if n >= HALF:
+                record_copy(n).start()
             wave = source_wave[lax.rem(grp, 2), n]
             electric = [[electric[c][z] + factor[z] * turn[c][z] for z in range(NZ)] for c in range(3)]
             electric[0] = [electric[0][z] + wave * counts[z] for z in range(NZ)]
@@ -637,9 +638,6 @@
             device_id=device(grp, j, 0),
             device_id_type=MESH,
         )
-
-    def own_share():
-        return pltpu.make_async_copy(shares.at[0], gathered.at[0], local_sem.at[3])
 
     def share_copy(i):
         return pltpu.make_async_remote_copy(
@@ -678,7 +676,7 @@
             gradient = gradient - (1.0 / DT) * (slope[0] + slope[1])[:TX, :TY]
             if n == 0:
                 tiles[0] = gradient
-                for j in far_first(n_gx)[:-1]:
+                for j in line_far_first():
                     tile_copy(j).start()
             turn = curl_up([[factor[z] * electric[c][z] for z in range(NZ)] for c in range(3)])
             magnetic = [[magnetic[c][z] + unit * turn[c][z] for z in range(NZ)] for c in range(3)]
@@ -709,20 +707,17 @@
             rest = rest - part.astype(F32)
         for i in range(4 * n_gy):
             shares[i] = total[SHARE * i : SHARE * (i + 1)]
-        own_share().start()
+        gathered[0] = total[:SHARE]
         pl.semaphore_wait(fourth_round, 1)
-        for j in far_first(n_gy):
-            for lane in (2, 1, 3, 0):
-                if lane + j:
-                    share_copy(lane * n_gy + j).start()
-
-    for lane in (2, 3):
-        start = lax.rem(grp + 4 - lane, 4) * n_gy
-        each(start + jnp.where(start == 0, 1, 0), start + n_gy, lambda i: share_copy(i).wait_recv())
+        for d in far_first(n_gy // 2):
+            for lane in (0, 1, 3, 2):
+                for other in (0, 1):
+                    if d or lane or other:
+                        place = lax.rem(gy - gy % 2 + (gy + other) % 2 + 2 * d, n_gy)
+                        share_copy(lane * n_gy + lax.rem(place - gy + n_gy, n_gy)).start()
 
     for i, copy in enumerate(rim_copies()):
         sent(i, copy.wait_send)
-    state_copy().wait()
 
     @pl.when(forward)
     def _():
@@ -730,11 +725,8 @@
             copy.wait_send()
         for k in range(HALF - 1):
             whole_half(k).wait_send()
-        for n in range(STEPS):
-            if n < HALF:
-                kept_copy(n).wait()
-            else:
-                record_copy(n).wait_send()
+        for n in range(HALF, STEPS):
+            record_copy(n).wait_send()
 
     @pl.when(adjoint)
     def _():
@@ -749,18 +741,29 @@
             tile_copy(j).wait_send()
         for i in range(1, 4 * n_gy):
             share_copy(i).wait_send()
-        own_share().wait()
-
-
-def store(n_gy, fields, stored, gathered, fields_next, stored_next, design_grad):
-    fields_next[...] = fields[...]
-    stored_next[...] = stored[...]
-    total = jnp.zeros((SHARE, TY), F32)
+
+    for lane in (2, 3):
+        start = lax.rem(grp + 4 - lane, 4) * n_gy
+        each(start + jnp.where(start == 0, 1, 0), start + n_gy, lambda i: share_copy(i).wait_recv())
+
+
+def store(n_gy, fields, stored, gathered, fields_next, stored_next, design_grad, total, sem):
+    copies = [
+        pltpu.make_async_copy(fields, fields_next, sem.at[0]),
+        pltpu.make_async_copy(stored, stored_next, sem.at[1]),
+        pltpu.make_async_copy(total, design_grad, sem.at[2]),
+    ]
+    copies[0].start()
+    copies[1].start()
+    value = jnp.zeros((SHARE, TY), F32)
     for lane in (2, 3):
         start = lax.rem(lax.axis_index("grp") + 4 - lane, 4) * n_gy
         for j in range(n_gy):
-            total = total + gathered[start + j]
-    design_grad[...] = total
+            value = value + gathered[start + j]
+    total[...] = value
+    copies[2].start()
+    for copy in copies:
+        copy.wait()
 
 
 def local(fields, stored, material, design, mat_eps, mat_chi, source_wave, source_cells, monitor_cells, owners):
@@ -772,12 +775,12 @@
     outs = pl.pallas_call(
         functools.partial(kernel, n_gx, n_gy),
         out_shape=(
-            jax.ShapeDtypeStruct((6, NZ, TX, TY), F32),
-            jax.ShapeDtypeStruct((HALF, 6, NZ, TX, TY), BF16),
-            jax.ShapeDtypeStruct((4 * n_gy, SHARE, TY), F32),
+            pltpu.VMEM((6, NZ, TX, TY), F32),
+            pltpu.VMEM((HALF, 6, NZ, TX, TY), BF16),
+            pltpu.VMEM((4 * n_gy, SHARE, TY), F32),
         ),
         in_specs=[hbm] * 10,
-        out_specs=(hbm, hbm, hbm),
+        out_specs=(vmem, vmem, vmem),
         scratch_shapes=[
             pltpu.VMEM((6, NZ, TX, TY), F32),
             pltpu.VMEM((HALF, 6, NZ, TX, TY), BF16),
@@ -805,8 +808,7 @@
             pltpu.VMEM((6, TX, TY), BF16),
             pltpu.VMEM((2, 3, TX, TY), BF16),
             pltpu.VMEM((TX, TY), BF16),
-            pltpu.VMEM((STEPS, 6, NZ, TX, TY), BF16),
-            pltpu.VMEM((6, NZ, TX, TY), F32),
+            pltpu.VMEM((HALF, 6, NZ, TX, TY), BF16),
             pltpu.VMEM((NZ * EX, EY), F32),
             pltpu.VMEM((4 * n_gy * SHARE, n_gx * TX), BF16),
             pltpu.VMEM((n_gx, TX, TY), F32),
@@ -831,7 +833,6 @@
             dma((n_gx,)),
             dma((4 * n_gy,)),
             dma((4 * n_gy,)),
-            dma((4,)),
             dma((10,)),
         ],
         compiler_params=pltpu.CompilerParams(
@@ -858,8 +859,9 @@
             jax.ShapeDtypeStruct((SHARE, TY), F32),
         ),
         in_specs=[vmem] * 3,
-        out_specs=(vmem,) * 3,
-        compiler_params=pltpu.CompilerParams(vmem_limit_bytes=56 * 1024 * 1024),
+        out_specs=(hbm,) * 3,
+        scratch_shapes=[pltpu.VMEM((SHARE, TY), F32), dma((3,))],
+        compiler_params=pltpu.CompilerParams(vmem_limit_bytes=8 * 1024 * 1024),
         name="store",
     )(*outs)
     return fields_next[None], stored_next[None], design_grad

time: 39.7 us -> 38.4 us (0.967)
  Pallas kernels: 38.9 us -> 37.6 us
    pallas_call x1, Pallas kernels: 1.63 us -> 0.7 us  [local(): pl.pallas_call(functools.partial(store, n_gy), out_shape=(jax.ShapeDtypeS...]
where the time goes in v5:
time: 38.4 us; the launch traced here: 38.3 us
  Pallas kernels  37.6 us (98%)
  between operations  0.64 us (2%)
    pallas_call x1, Pallas kernels, local(): pl.pallas_call(functools.partial(kernel, n_gx, n_gy), out_shape=(pltpu.VM...  36.9 us

profile of v5, /device:TPU:1, one launch (start us, length us, event | category | flops | bytes accessed | tf_op | source)
XLA Modules:
  0.0 38.3 jit_solution(11294945773225249173)
XLA Ops:
  0.6 36.9 %interval.1 = (f32[6,2,16,128]{3,2,1,0:T(8,128)S(1)}, bf16[2,6,2,16,128]{4,3,2,1,0:T(8,128)(2,1)S(1)}, f32[32,4,128]{2,1,0:T(4,128)S(1)}) custom-call(f32[6,2,16,128]{3,2,1,0:T(8,128)} %bitcast.7, bf16[2,6,2,16,128]{4,3,2,1,0:T(8,128)(2,1)} %bitcast.8, s32[2,16,128]{2,1,0:T(8,128)} %material_in.1, f32[16,128]{1,0:T(8,128)} %design_in.1, f32[4]{0:T(128)} %mat_eps_in.1, ...), custom_call_target="tpu_custom_call" | custom-call | tf_op jit(solution)/shard_map/interval/pallas_call | solution.py:775
  37.6 0.7 %store.1 = (f32[6,2,16,128]{3,2,1,0:T(8,128)}, bf16[2,6,2,16,128]{4,3,2,1,0:T(8,128)(2,1)}, f32[4,128]{1,0:T(4,128)}) custom-call(f32[6,2,16,128]{3,2,1,0:T(8,128)S(1)} %get-tuple-element.9.fields, bf16[2,6,2,16,128]{4,3,2,1,0:T(8,128)(2,1)S(1)} %get-tuple-element.10.stored, f32[32,4,128]{2,1,0:T(4,128)S(1)} %get-tuple-element.11.gathered), custom_call_target="tpu_custom_call" | custom-call | tf_op jit(solution)/shard_map/store/pallas_call | solution.py:854

commit v6 on v5

--- a/solution.py
+++ b/solution.py
@@ -24,10 +24,6 @@
 SHARE = 4
 
 AROUND = ((-1, 0), (1, 0), (0, -1), (0, 1), (-1, -1), (-1, 1), (1, -1), (1, 1))
-
-
-def far_first(length):
-    return sorted(range(length), key=lambda j: -min(j, length - j))
 
 
 def iota(shape, axis):
@@ -223,14 +219,6 @@
     def in_row(d):
         return {"grp": grp, "gx": gx - gx % side + (gx + d) % side, "gy": gy}
 
-    def line_far_first():
-        def across(place, c):
-            return (place, place + 1 - 2 * (place % 2), (place + 2) % 4, 3 - place)[c]
-
-        codes = [(a, b) for a in range(n_gx // side) for b in range(side)]
-        for a, b in sorted(codes, key=lambda code: -sum(code))[:-1]:
-            yield lax.rem(across(gx // side, a) * side + across(gx % side, b) - gx + n_gx, n_gx)
-
     def in_pair(d, other):
         return {"grp": grp, "gx": gx, "gy": lax.rem(gy - gy % 2 + (gy + other) % 2 + 2 * d + n_gy, n_gy)}
 
@@ -421,6 +409,65 @@
         col_out[...] = pack_columns(planes)
         for i in range(8):
             row_out[0, i], row_out[1, i] = pack_rows(planes[2 * i], planes[2 * i + 1])
+
+    def tally(a, b):
+        return lax.dot_general(a, b, (((1,), (1,)), ((), ())), preferred_element_type=F32)
+
+    def count_cells():
+        row = iota((NZ * EX, TY), 0)
+        depth = jnp.where(row >= EX, 1, 0)
+        row = row - depth * EX
+        x = gx * TX + jnp.where(row < TX + RIM, row, row - EX)
+        sought_x = jnp.where((x >= 0) & (x < n_gx * TX), depth * (n_gx * TX) + x, -1)
+        column = iota((TY, TY), 0)
+        sought_y = gy * TY + column
+        sought_high = sought_y[:8] + TY
+        sought_low = sought_y[TY - 8 :] - TY
+        listed = jnp.where(forward, source_cells[...], monitor_cells[...])
+        listed_x = listed // (n_gy * TY)
+        listed_y = listed % (n_gy * TY)
+
+        def hits(found):
+            return jnp.where(found, 1.0, 0.0)
+
+        def wide(m, i, rows):
+            return jnp.broadcast_to(m[i : i + 1], (rows, TY))
+
+        entries = listed.shape[0]
+        rows_hit = jnp.concatenate(
+            [hits(wide(listed_x, i, NZ * EX) == sought_x) for i in range(entries)], axis=1
+        ).astype(BF16)
+        columns_hit = jnp.concatenate(
+            [hits(wide(listed_y, i, TY) == sought_y) for i in range(entries)], axis=1
+        ).astype(BF16)
+        high_hit = jnp.concatenate([hits(wide(listed_y, i, 8) == sought_high) for i in range(entries)], axis=1)
+        low_hit = jnp.concatenate([hits(wide(listed_y, i, 8) == sought_low) for i in range(entries)], axis=1)
+        rim_hit = jnp.concatenate(
+            [high_hit, jnp.zeros((TY - 16, entries * TY), F32), low_hit], axis=0
+        ).astype(BF16)
+
+        counts_ref[...] = jnp.concatenate([tally(rows_hit, columns_hit), tally(rows_hit, rim_hit)], axis=1)
+
+    def choose_tiles():
+        lanes = owners.shape[1]
+        pick = iota((TX, lanes), 1) == iota((TX, lanes), 0) * n_gy + gy
+        coarse, fine = [], []
+        for j in range(n_gx):
+            line = jnp.broadcast_to(owners[pl.ds(lax.rem(gx - j + n_gx, n_gx), 1)], (TX, lanes))
+            line = jnp.where(pick, line, 0)
+            part = line // 64 * 64
+            coarse.append(part.astype(F32))
+            fine.append((line - part).astype(F32))
+        rows = 4 * n_gy * SHARE
+        ones = jnp.ones((rows, lanes), BF16)
+        owner = tally(ones, jnp.concatenate(coarse, axis=0).astype(BF16))
+        owner = owner + tally(ones, jnp.concatenate(fine, axis=0).astype(BF16))
+        place = iota((rows, n_gx * TX), 0)
+        share = place // SHARE
+        lane = (grp + share // n_gy) % 4
+        spot = (gy + share % n_gy) % n_gy
+        wanted = ((lane * n_gx + gx) * n_gy + spot) * SHARE + place % SHARE
+        chosen[...] = jnp.where(owner == wanted.astype(F32), 1.0, 0.0).astype(BF16)
 
     stored_load = loads.pop(1)
 
@@ -445,15 +492,13 @@
         pack_rims()
         whole_half(1).wait_send()
         whole_half(0).start()
+        count_cells()
 
     @pl.when(adjoint)
     def _():
         for load in loads:
             load.wait()
         pack_rims()
-        all_in()
-        send_rims()
-        begin_second()
         stored_load.wait()
         for k in range(HALF - 1, -1, -1):
             planes = half_planes(k, 6)
@@ -463,67 +508,18 @@
                 two = pack_rows(planes[4 * i + 2], planes[4 * i + 3])
                 for side in range(2):
                     rowh_out[side, k, i] = jnp.concatenate([one[side], two[side]], axis=0).astype(BF16)
+        all_in()
+        send_rims()
+        begin_second()
+        for k in range(HALF - 1, -1, -1):
             for i in range(7, -1, -1):
                 sent(i, half_copy(k, i).start)
-
-    row = iota((NZ * EX, TY), 0)
-    depth = jnp.where(row >= EX, 1, 0)
-    row = row - depth * EX
-    x = gx * TX + jnp.where(row < TX + RIM, row, row - EX)
-    sought_x = jnp.where((x >= 0) & (x < n_gx * TX), depth * (n_gx * TX) + x, -1)
-    column = iota((TY, TY), 0)
-    sought_y = gy * TY + column
-    sought_high = sought_y[:8] + TY
-    sought_low = sought_y[TY - 8 :] - TY
-    listed = jnp.where(forward, source_cells[...], monitor_cells[...])
-    listed_x = listed // (n_gy * TY)
-    listed_y = listed % (n_gy * TY)
-
-    def hits(found):
-        return jnp.where(found, 1.0, 0.0)
-
-    def wide(m, i, rows):
-        return jnp.broadcast_to(m[i : i + 1], (rows, TY))
-
-    entries = listed.shape[0]
-    rows_hit = jnp.concatenate(
-        [hits(wide(listed_x, i, NZ * EX) == sought_x) for i in range(entries)], axis=1
-    ).astype(BF16)
-    columns_hit = jnp.concatenate(
-        [hits(wide(listed_y, i, TY) == sought_y) for i in range(entries)], axis=1
-    ).astype(BF16)
-    high_hit = jnp.concatenate([hits(wide(listed_y, i, 8) == sought_high) for i in range(entries)], axis=1)
-    low_hit = jnp.concatenate([hits(wide(listed_y, i, 8) == sought_low) for i in range(entries)], axis=1)
-    rim_hit = jnp.concatenate(
-        [high_hit, jnp.zeros((TY - 16, entries * TY), F32), low_hit], axis=0
-    ).astype(BF16)
-
-    def tally(a, b):
-        return lax.dot_general(a, b, (((1,), (1,)), ((), ())), preferred_element_type=F32)
-
-    counts_ref[...] = jnp.concatenate([tally(rows_hit, columns_hit), tally(rows_hit, rim_hit)], axis=1)
-
-    @pl.when(adjoint)
-    def _():
-        lanes = owners.shape[1]
-        pick = iota((TX, lanes), 1) == iota((TX, lanes), 0) * n_gy + gy
-        coarse, fine = [], []
-        for j in range(n_gx):
-            line = jnp.broadcast_to(owners[pl.ds(lax.rem(gx - j + n_gx, n_gx), 1)], (TX, lanes))
-            line = jnp.where(pick, line, 0)
-            part = line // 64 * 64
-            coarse.append(part.astype(F32))
-            fine.append((line - part).astype(F32))
-        rows = 4 * n_gy * SHARE
-        ones = jnp.ones((rows, lanes), BF16)
-        owner = tally(ones, jnp.concatenate(coarse, axis=0).astype(BF16))
-        owner = owner + tally(ones, jnp.concatenate(fine, axis=0).astype(BF16))
-        place = iota((rows, n_gx * TX), 0)
-        share = place // SHARE
-        lane = (grp + share // n_gy) % 4
-        spot = (gy + share % n_gy) % n_gy
-        wanted = ((lane * n_gx + gx) * n_gy + spot) * SHARE + place % SHARE
-        chosen[...] = jnp.where(owner == wanted.astype(F32), 1.0, 0.0).astype(BF16)
+        for copy in thin_copies():
+            copy.wait_recv()
+        for i in range(7, -1, -1):
+            sent(i, thin_copy(i).start)
+        count_cells()
+        choose_tiles()
 
     row = iota((EX, EY), 0)
     column = iota((EX, EY), 1)
@@ -536,10 +532,6 @@
 
     @pl.when(adjoint)
     def _():
-        for copy in thin_copies():
-            copy.wait_recv()
-        for i in range(7, -1, -1):
-            sent(i, thin_copy(i).start)
         end_second()
 
     @pl.when(forward)
@@ -676,8 +668,12 @@
             gradient = gradient - (1.0 / DT) * (slope[0] + slope[1])[:TX, :TY]
             if n == 0:
                 tiles[0] = gradient
-                for j in line_far_first():
-                    tile_copy(j).start()
+                for place in range(n_gx):
+
+                    @pl.when(gx != place)
+                    def _():
+                        tile_copy(lax.rem(place - gx + n_gx, n_gx)).start()
+
             turn = curl_up([[factor[z] * electric[c][z] for z in range(NZ)] for c in range(3)])
             magnetic = [[magnetic[c][z] + unit * turn[c][z] for z in range(NZ)] for c in range(3)]
             turn = curl_down(magnetic)
@@ -709,12 +705,20 @@
             shares[i] = total[SHARE * i : SHARE * (i + 1)]
         gathered[0] = total[:SHARE]
         pl.semaphore_wait(fourth_round, 1)
-        for d in far_first(n_gy // 2):
-            for lane in (0, 1, 3, 2):
-                for other in (0, 1):
-                    if d or lane or other:
-                        place = lax.rem(gy - gy % 2 + (gy + other) % 2 + 2 * d, n_gy)
-                        share_copy(lane * n_gy + lax.rem(place - gy + n_gy, n_gy)).start()
+        pair, count = gy // 2, n_gy // 2
+        first = jnp.where(pair == 0, count // 2, count - pair)
+        for step_on in range(count - 1):
+            away = lax.rem(first - 1 + step_on, count - 1) + 1
+            for lane in range(4):
+                ahead = lax.rem(lane + 4 - grp, 4) * n_gy
+                for core in (1, 0):
+                    place = 2 * lax.rem(pair + away, count) + core
+                    share_copy(ahead + lax.rem(place - gy + n_gy, n_gy)).start()
+        for lane in range(4):
+            for other in (0, 1):
+                if lane or other:
+                    place = gy - gy % 2 + (gy + other) % 2
+                    share_copy(lane * n_gy + lax.rem(place - gy + n_gy, n_gy)).start()
 
     for i, copy in enumerate(rim_copies()):
         sent(i, copy.wait_send)

time: 38.4 us -> 37.8 us (0.984)
  Pallas kernels: 37.6 us -> 37 us
    pallas_call x1, Pallas kernels: 36.9 us -> 36.3 us  [local(): pl.pallas_call(functools.partial(kernel, n_gx, n_gy), out_shape=(pltpu.VM...]
where the time goes in v6:
time: 37.8 us; the launch traced here: 37.6 us
  Pallas kernels  37 us (98%)
  between operations  0.64 us (2%)
    pallas_call x1, Pallas kernels, local(): pl.pallas_call(functools.partial(kernel, n_gx, n_gy), out_shape=(pltpu.VM...  36.3 us

profile of v6, /device:TPU:1, one launch (start us, length us, event | category | flops | bytes accessed | tf_op | source)
XLA Modules:
  0.0 37.6 jit_solution(9025046877104235239)
XLA Ops:
  0.6 36.3 %interval.1 = (f32[6,2,16,128]{3,2,1,0:T(8,128)S(1)}, bf16[2,6,2,16,128]{4,3,2,1,0:T(8,128)(2,1)S(1)}, f32[32,4,128]{2,1,0:T(4,128)S(1)}) custom-call(f32[6,2,16,128]{3,2,1,0:T(8,128)} %bitcast.7, bf16[2,6,2,16,128]{4,3,2,1,0:T(8,128)(2,1)} %bitcast.8, s32[2,16,128]{2,1,0:T(8,128)} %material_in.1, f32[16,128]{1,0:T(8,128)} %design_in.1, f32[4]{0:T(128)} %mat_eps_in.1, ...), custom_call_target="tpu_custom_call" | custom-call | tf_op jit(solution)/shard_map/interval/pallas_call | solution.py:779
  36.9 0.7 %store.1 = (f32[6,2,16,128]{3,2,1,0:T(8,128)}, bf16[2,6,2,16,128]{4,3,2,1,0:T(8,128)(2,1)}, f32[4,128]{1,0:T(4,128)}) custom-call(f32[6,2,16,128]{3,2,1,0:T(8,128)S(1)} %get-tuple-element.9.fields, bf16[2,6,2,16,128]{4,3,2,1,0:T(8,128)(2,1)S(1)} %get-tuple-element.10.stored, f32[32,4,128]{2,1,0:T(4,128)S(1)} %get-tuple-element.11.gathered), custom_call_target="tpu_custom_call" | custom-call | tf_op jit(solution)/shard_map/store/pallas_call | solution.py:858

commit v7 on v6

--- a/solution.py
+++ b/solution.py
@@ -304,8 +304,11 @@
         chi = [lookup(kinds[z], mat_chi) for z in range(NZ)]
         return [fields[c, z] for c in range(6) for z in range(NZ)] + eps + chi
 
+    def half_planes_of(half, k, components):
+        return [half[k, c, z].astype(F32) for c in range(components) for z in range(NZ)]
+
     def half_planes(k, components):
-        return [stored[k, c, z].astype(F32) for c in range(components) for z in range(NZ)]
+        return half_planes_of(stored, k, components)
 
     def row_copy(i):
         return pltpu.make_async_remote_copy(
@@ -341,16 +344,16 @@
     def rim_copies():
         return [row_copy(0), row_copy(1), col_copy(2), col_copy(3)] + [corner_copy(i) for i in range(4, 8)]
 
-    def half_copy(k, i):
+    def half_copy(i):
         if i < 2:
-            src, dst = rowh_out.at[i, k], rowh_in.at[i, k]
+            src, dst = rowh_out.at[i], rowh_in.at[i]
         else:
-            src, dst = colh_out.at[k], colh_in.at[i - 2, k]
+            src, dst = colh_out, colh_in.at[i - 2]
         return pltpu.make_async_remote_copy(
             src_ref=src,
             dst_ref=dst,
-            send_sem=ownh_sem.at[k, i],
-            recv_sem=inh_sem.at[k, i],
+            send_sem=ownh_sem.at[i],
+            recv_sem=inh_sem.at[i],
             device_id=device(grp, *AROUND[i]),
             device_id_type=MESH,
         )
@@ -510,10 +513,9 @@
                     rowh_out[side, k, i] = jnp.concatenate([one[side], two[side]], axis=0).astype(BF16)
         all_in()
         send_rims()
+        for i in range(7, -1, -1):
+            sent(i, half_copy(i).start)
         begin_second()
-        for k in range(HALF - 1, -1, -1):
-            for i in range(7, -1, -1):
-                sent(i, half_copy(k, i).start)
         for copy in thin_copies():
             copy.wait_recv()
         for i in range(7, -1, -1):
@@ -646,13 +648,30 @@
         electric, magnetic = first, second
         gradient = jnp.zeros((TX, TY), F32)
         for n in range(STEPS - 1, -1, -1):
+            if n == 0:
+                whole_half(0).wait_recv()
+                tile = vectors(half_planes_of(half_in, 0, 6))
+                field = [[electric[c][z][:TX, :TY] for z in range(NZ)] for c in range(3)]
+                for z in range(NZ):
+                    divisor = eps[z][:TX, :TY] + chi[z][:TX, :TY] * square(tile[:3], z)
+                    product = sum(tile[3 + c][z] * field[c][z] for c in range(3))
+                    part = DT / divisor
+                    gradient = gradient - (1.0 / DT) * part * part * product
+                tiles[0] = gradient
+                for place in range(n_gx):
+
+                    @pl.when(gx != place)
+                    def _():
+                        tile_copy(lax.rem(place - gx + n_gx, n_gx)).start()
+
             if n >= HALF:
-                for i in range(8):
-                    received(i, half_copy(n - HALF, i).wait_recv)
+                if n == STEPS - 1:
+                    for i in range(8):
+                        received(i, half_copy(i).wait_recv)
                 snapshot = late_snapshot(n - HALF)
             else:
-                whole_half(n).wait_recv()
                 if n == HALF - 1:
+                    whole_half(n).wait_recv()
                     for i in range(8):
                         received(i, thin_copy(i).wait_recv)
                     packed = [colc_in[i].astype(F32) for i in range(6)]
@@ -665,15 +684,8 @@
                 for z in range(NZ)
             ]
             slope = [factor[z] * factor[z] * inner[z] for z in range(NZ)]
-            gradient = gradient - (1.0 / DT) * (slope[0] + slope[1])[:TX, :TY]
-            if n == 0:
-                tiles[0] = gradient
-                for place in range(n_gx):
-
-                    @pl.when(gx != place)
-                    def _():
-                        tile_copy(lax.rem(place - gx + n_gx, n_gx)).start()
-
+            if n:
+                gradient = gradient - (1.0 / DT) * (slope[0] + slope[1])[:TX, :TY]
             turn = curl_up([[factor[z] * electric[c][z] for z in range(NZ)] for c in range(3)])
             magnetic = [[magnetic[c][z] + unit * turn[c][z] for z in range(NZ)] for c in range(3)]
             turn = curl_down(magnetic)
@@ -682,13 +694,6 @@
                 [electric[c][z] + weight[z] * past[c][z] - step * turn[c][z] for z in range(NZ)] for c in range(3)
             ]
         finish(electric, magnetic)
-
-    def each(low, high, act):
-        def body(i, carry):
-            act(i)
-            return carry
-
-        lax.fori_loop(low, high, body, 0)
 
     @pl.when(adjoint)
     def _():
@@ -734,9 +739,8 @@
 
     @pl.when(adjoint)
     def _():
-        for k in range(HALF):
-            for i in range(8):
-                sent(i, half_copy(k, i).wait_send)
+        for i in range(8):
+            sent(i, half_copy(i).wait_send)
         for i in range(8):
             sent(i, thin_copy(i).wait_send)
         for n in range(HALF, STEPS):
@@ -748,7 +752,9 @@
 
     for lane in (2, 3):
         start = lax.rem(grp + 4 - lane, 4) * n_gy
-        each(start + jnp.where(start == 0, 1, 0), start + n_gy, lambda i: share_copy(i).wait_recv())
+        pl.when(start > 0)(share_copy(start).wait_recv)
+        for j in range(1, n_gy):
+            share_copy(start + j).wait_recv()
 
 
 def store(n_gy, fields, stored, gathered, fields_next, stored_next, design_grad, total, sem):
@@ -818,10 +824,10 @@
             pltpu.VMEM((n_gx, TX, TY), F32),
             pltpu.VMEM((4 * n_gy, SHARE, TY), F32),
             dma((8,)),
-            dma((HALF, 8)),
+            dma((8,)),
             dma((HALF,)),
             dma((8,)),
-            dma((HALF, 8)),
+            dma((8,)),
             dma((HALF,)),
             dma((8,)),
             dma((8,)),

time: 37.8 us -> 37.6 us (level)
  no operation moved by 1% of the time
where the time goes in v7:
time: 37.6 us; the launch traced here: 37.5 us
  Pallas kernels  36.8 us (98%)
  between operations  0.64 us (2%)
    pallas_call x1, Pallas kernels, local(): pl.pallas_call(functools.partial(kernel, n_gx, n_gy), out_shape=(pltpu.VM...  36.1 us

profile of v7, /device:TPU:1, one launch (start us, length us, event | category | flops | bytes accessed | tf_op | source)
XLA Modules:
  0.0 37.5 jit_solution(9216582085416875090)
XLA Ops:
  0.6 36.1 %interval.1 = (f32[6,2,16,128]{3,2,1,0:T(8,128)S(1)}, bf16[2,6,2,16,128]{4,3,2,1,0:T(8,128)(2,1)S(1)}, f32[32,4,128]{2,1,0:T(4,128)S(1)}) custom-call(f32[6,2,16,128]{3,2,1,0:T(8,128)} %bitcast.7, bf16[2,6,2,16,128]{4,3,2,1,0:T(8,128)(2,1)} %bitcast.8, s32[2,16,128]{2,1,0:T(8,128)} %material_in.1, f32[16,128]{1,0:T(8,128)} %design_in.1, f32[4]{0:T(128)} %mat_eps_in.1, ...), custom_call_target="tpu_custom_call" | custom-call | tf_op jit(solution)/shard_map/interval/pallas_call | solution.py:785
  36.8 0.7 %store.1 = (f32[6,2,16,128]{3,2,1,0:T(8,128)}, bf16[2,6,2,16,128]{4,3,2,1,0:T(8,128)(2,1)}, f32[4,128]{1,0:T(4,128)}) custom-call(f32[6,2,16,128]{3,2,1,0:T(8,128)S(1)} %get-tuple-element.9.fields, bf16[2,6,2,16,128]{4,3,2,1,0:T(8,128)(2,1)S(1)} %get-tuple-element.10.stored, f32[32,4,128]{2,1,0:T(4,128)S(1)} %get-tuple-element.11.gathered), custom_call_target="tpu_custom_call" | custom-call | tf_op jit(solution)/shard_map/store/pallas_call | solution.py:864
